TPU v7x, 512 devices: a whole 4x4x16 slice. The times are simulated.
512 devices in a mesh: tensor: 8 (over x_hi, y), dp: 64 (over z, x_lo, core).
Axes of the slice: x: 4 (x_hi: 2, x_lo: 2; x = x_hi * 2 + x_lo), y: 4, z: 16, core: 2. Of those that a mesh axis runs over, the one named last changes fastest.
Arguments:
- activations: bfloat16 [3, 8192, 4096], P(None, 'dp'), may hold values from -16 to 16
- kv_grads: bfloat16 [3, 8192, 2048], P(None, 'dp', 'tensor'), may hold values from -6 to 6
- norm_gain: float32 [4096], replicated, may hold values from 0.25 to 3.5
- master: float32 [4096, 2048], P('dp', 'tensor'), may hold values from -0.09375 to 0.09375
- moment_one: float32 [4096, 2048], P('dp', 'tensor'), may hold values from -6 to 6
- moment_two: float32 [4096, 2048], P('dp', 'tensor'), may hold values from 0.5 to 5
- lengths: int32 [3, 64], P(None, 'dp'), may hold values from 16 to 128, as said below
- labels: int32 [3, 8192], P(None, 'dp'), may hold values from -100 to 31999
Outputs:
- input_grads: bfloat16 [3, 8192, 4096], P(None, 'dp', 'tensor')
- new_master: float32 [4096, 2048], P('dp', 'tensor')
- new_moment_one: float32 [4096, 2048], P('dp', 'tensor')
- new_moment_two: float32 [4096, 2048], P('dp', 'tensor')
Inputs may be any that keep to these rules, and one draw needn't show every extreme that they name: `lengths`: in every micro-batch one dp index has all 128 positions live and another has 16.
All inputs are finite; a program needn't handle non-finite values.
Results may differ from a plain program's by a relative error of at most 0.019.
Values may be sent and summed in bfloat16 or wider, within the bound.
No kernel may reach another device: no remote copies, remote signals or barrier semaphores. Data moves between devices by JAX's collectives and lax.ppermute only.
A program may use at most 64 MiB of HBM per device.

v0:
```python
import jax
import jax.numpy as jnp
from jax import lax
from jax.sharding import PartitionSpec as P

norm_eps = 1e-05
beta_one = 0.9
beta_two = 0.95
learn_rate = 0.002
adam_eps = 1e-08
adam_step = 100


def column_term(left, right):
    return lax.dot_general(
        left, right, (((0,), (0,)), ((), ())), preferred_element_type=jnp.float32
    )


def on_device(activations, kv_grads, norm_gain, master, moment_one, moment_two, lengths, labels):
    batches, tok_rows, features = activations.shape
    columns = kv_grads.shape[2]
    position = lax.broadcasted_iota(jnp.int32, (batches, tok_rows), 1)
    live_mask = (position < lengths) & (labels != -100)
    kv_live = jnp.where(live_mask[:, :, None], kv_grads, jnp.zeros_like(kv_grads))
    wide_rows = activations.astype(jnp.float32)
    row_scale = lax.rsqrt(jnp.mean(wide_rows * wide_rows, axis=-1, keepdims=True) + norm_eps)
    unit_rows = wide_rows * row_scale
    normed = (unit_rows * norm_gain).astype(jnp.bfloat16)
    flat_normed = normed.reshape(batches * tok_rows, features)
    flat_kv = kv_live.reshape(batches * tok_rows, columns)
    weight_grad = lax.psum_scatter(
        column_term(flat_normed, flat_kv), "dp", scatter_dimension=0, tiled=True
    )
    weights = master.astype(jnp.bfloat16)
    group_terms = lax.dot_general(
        flat_kv,
        lax.all_gather(weights, "dp", axis=0, tiled=True),
        (((1,), (1,)), ((), ())),
        preferred_element_type=jnp.float32,
    )
    group_terms = group_terms.reshape(batches, tok_rows, features)
    share_width = features // lax.axis_size("tensor")
    offset = lax.axis_index("tensor") * share_width
    pieces = []
    for micro_step in range(batches):
        summed = lax.psum(group_terms[micro_step].astype(jnp.bfloat16), "tensor").astype(
            jnp.float32
        )
        scaled = summed * norm_gain
        row_inner = jnp.mean(scaled * unit_rows[micro_step], axis=-1, keepdims=True)
        full_grad = row_scale[micro_step] * (scaled - unit_rows[micro_step] * row_inner)
        pieces.append(lax.dynamic_slice_in_dim(full_grad, offset, share_width, 1))
    input_grads = jnp.stack(pieces, axis=0).astype(jnp.bfloat16)
    mean_grad = weight_grad / lax.axis_size("dp") ** 0.5
    new_moment_one = beta_one * moment_one + (1.0 - beta_one) * mean_grad
    new_moment_two = beta_two * moment_two + (1.0 - beta_two) * mean_grad * mean_grad
    first_fixed = new_moment_one / (1.0 - beta_one**adam_step)
    second_fixed = new_moment_two / (1.0 - beta_two**adam_step)
    new_master = master - learn_rate * first_fixed / (jnp.sqrt(second_fixed) + adam_eps)
    return (input_grads, new_master, new_moment_one, new_moment_two)


def solution(mesh):
    return jax.shard_map(
        on_device,
        mesh=mesh,
        in_specs=(
            P(None, "dp", None),
            P(None, "dp", "tensor"),
            P(),
            P("dp", "tensor"),
            P("dp", "tensor"),
            P("dp", "tensor"),
            P(None, "dp"),
            P(None, "dp"),
        ),
        out_specs=(
            P(None, "dp", "tensor"),
            P("dp", "tensor"),
            P("dp", "tensor"),
            P("dp", "tensor"),
        ),
        check_vma=False,
    )
```

profile of v0, /device:TPU:32, one launch (start us, length us, event | category | flops | bytes accessed | tf_op | source)
XLA Modules:
  0.0 502.6 jit_solution(16839813376821470745)
XLA Ops:
  7.2 0.0 copy-start.1
  7.2 0.0 copy-start.8
  7.2 0.0 copy-start.9
  7.2 0.0 copy-start.5
  7.2 0.0 reduce-scatter.2.cloned.1.call-start
  7.3 2.7 fusion
  10.0 0.0 copy-done.8
  10.0 0.0 copy-done.9
  10.0 0.1 fusion.11
  10.1 1.0 broadcast_select_fusion
  11.1 0.0 copy-done.1
  11.2 3.4 convolution_bitcast_fusion
  14.6 0.0 reduce-scatter.2.cloned.1.call-update
  14.6 0.0 all-gather.2.cloned.1.call-start
  14.7 229.4 %reduce-scatter.2.cloned.1.call-done = f32[64,256]{1,0:T(8,128)} async-done(((f32[4096,256]{1,0:T(8,128)}), f32[64,256]{1,0:T(8,128)}) %reduce-scatter.2.cloned.1.call-update) | async-done | bytes 65552 | tf_op jit(solution)/shard_map/reduce_scatter | solution.py:32
  244.1 0.0 copy-done.3
  244.1 1.5 divide_subtract_fusion
  245.6 0.0 all-gather.2.cloned.1.call-update
  245.6 0.0 all-reduce.3.cloned.1.call-start
  245.7 127.2 %all-gather.2.cloned.1.call-done = bf16[4096,256]{1,0:T(8,128)(2,1)} async-done(((bf16[64,256]{1,0:T(8,128)(2,1)}), bf16[4096,256]{1,0:T(8,128)(2,1)}) %all-gather.2.cloned.1.call-update) | async-done | bytes 2097168 | tf_op jit(solution)/shard_map/all_gather | solution.py:38
  372.9 2.6 convolution_convert_fusion
  375.5 1.7 fusion.12
  377.2 0.0 all-reduce.3.cloned.1.call-update
  377.2 0.7 copy-done.7
  377.9 0.8 convert_multiply_fusion
  378.8 2.7 copy-done
  381.4 2.4 slice_bitcast_fusion.2
  383.9 104.6 %all-reduce.3.cloned.1.call-done = (bf16[128,4096]{1,0:T(8,128)(2,1)}, bf16[128,4096]{1,0:T(8,128)(2,1)}, bf16[128,4096]{1,0:T(8,128)(2,1)}) async-done(((bf16[128,4096]{1,0:T(8,128)(2,1)}, bf16[128,4096]{1,0:T(8,128)(2,1)}, bf16[128,4096]{1,0:T(8,128)(2,1)}), (bf16[128,4096]{1,0:T(8,128)(2,1)}, bf16[128,4096]{1,0:T(8,128)(2,1)}, bf16[128,4096]{1,0:T(8,128)(2,1)})) %all-reduce.3.cloned.1.call-update) | async-done | bytes 3145744 | tf_op jit(solution)/shard_map/psum | solution.py:47
  488.5 4.6 multiply_reduce_fusion.2
  493.1 1.1 fusion.10
  494.2 1.1 fusion.8
  495.3 0.8 pad_maximum_fusion
  (15 shorter events, 0.0 us)
Async XLA Ops:
  7.2 4.0 copy-start.1
  7.2 2.8 copy-start.8
  7.2 2.8 copy-start.9
  7.2 4.0 copy-start.5
  7.2 236.8 %reduce-scatter.2.cloned.1.call-start = ((), (), s32[]{:S(2)}) async-start(), calls=%async_computation.2 | async-start | bytes 4259840 | tf_op jit(solution)/shard_map/reduce_scatter | solution.py:32
  10.0 4.6 copy-start.6
  14.6 229.5 %copy-start.2 = (f32[64,256]{1,0:T(8,128)S(1)}, f32[64,256]{1,0:T(8,128)}, u32[]{:S(2)}) copy-start(f32[64,256]{1,0:T(8,128)} %param.11) | copy-start | bytes 196612
  14.6 229.5 %copy-start.3 = (f32[64,256]{1,0:T(8,128)S(1)}, f32[64,256]{1,0:T(8,128)}, u32[]{:S(2)}) copy-start(f32[64,256]{1,0:T(8,128)} %param.12) | copy-start | bytes 196612
  14.6 229.5 %copy-start.4 = (f32[64,256]{1,0:T(8,128)S(1)}, f32[64,256]{1,0:T(8,128)}, u32[]{:S(2)}) copy-start(f32[64,256]{1,0:T(8,128)} %param.13) | copy-start | bytes 196612
  14.6 358.3 %all-gather.2.cloned.1.call-start = ((), (), s32[]{:S(2)}) async-start(), calls=%async_computation.1 | async-start | bytes 2129920 | tf_op jit(solution)/shard_map/all_gather | solution.py:38
  245.6 242.9 %all-reduce.3.cloned.1.call-start = ((), (), s32[]{:S(2)}) async-start(), calls=%async_computation.3 | async-start | bytes 6291456 | tf_op jit(solution)/shard_map/psum | solution.py:47
  377.2 0.7 copy-start.7
  378.7 2.7 copy-start
Sparse Core Ops, SparseCore 0:
  14.7 229.2 reduce-scatter.1
  247.0 125.8 all-gather.1
  377.4 111.0 all-reduce.2
where the time goes:
time: 503 us
  waiting for transfers between devices  461 us (92%)
  between operations  13.9 us (3%)
  other arithmetic  13.8 us (3%)
  local copies, waits for them, and re-layouts  7.51 us (1%)
  matrix products  6.01 us (1%)
    reduce_scatter x1, waiting for transfers between devices, on_device(): lax.psum_scatter(column_term(flat_normed, flat_kv), 'dp', scatter_dimensi...  229 us
    all_gather x1, waiting for transfers between devices, on_device(): lax.all_gather(weights, 'dp', axis=0, tiled=True)  127 us
    psum x1, waiting for transfers between devices, on_device(): lax.psum(group_terms[micro_step].astype(jnp.bfloat16), 'tensor')  105 us
  transfers between devices with their start and end apart: 3, of which 3 were waited for; matrix products, arithmetic and copies ran while one was open for 1% of the time, Pallas kernels for 0%

commit v1 on v0

v1 whole, which is shorter than its diff:
```python
import jax
import jax.numpy as jnp
from jax import lax
from jax.sharding import Mesh, PartitionSpec as P

norm_eps = 1e-05
beta_one = 0.9
beta_two = 0.95
learn_rate = 0.002
adam_eps = 1e-08
adam_step = 100

TENSOR = ("x_hi", "y")
DP = ("z", "x_lo", "core")
SIZES = (2, 4, 16, 2, 2)
SWAP = ((0, 1), (1, 0))


def slice_owner_pairs():
    pairs = []
    for member in range(8):
        for plane in range(16):
            for quad in range(4):
                slice_of, low = plane // 2, plane % 2
                source = (member * 16 + plane) * 4 + quad
                target = (slice_of * 16 + 2 * member + low) * 4 + quad
                pairs.append((source, target))
    return pairs


def add_pair(mine, theirs):
    return mine.astype(jnp.float32) + theirs.astype(jnp.float32)


def on_device(activations, kv_grads, norm_gain, master, moment_one, moment_two, lengths, labels):
    batches, tok_rows, features = activations.shape
    columns = kv_grads.shape[2]
    tokens = batches * tok_rows
    x_at, core_at = lax.axis_index("x_lo"), lax.axis_index("core")
    member = lax.axis_index(TENSOR)

    moved = lax.ppermute(master.astype(jnp.bfloat16), TENSOR + DP, slice_owner_pairs())
    spread = jnp.broadcast_to(moved[None], (16,) + moved.shape)
    own_quarter = lax.all_to_all(spread, "z", 0, 0)
    x_quarter = lax.ppermute(own_quarter, "x_lo", SWAP)
    core_quarter = lax.ppermute(own_quarter, "core", SWAP)
    far_quarter = lax.ppermute(x_quarter, "core", SWAP)
    kv_all = lax.all_gather(kv_grads.reshape(tokens, columns), TENSOR, axis=0)

    position = lax.broadcasted_iota(jnp.int32, (batches, tok_rows), 1)
    live_mask = (position < lengths) & (labels != -100)
    kv_live = jnp.where(live_mask[:, :, None], kv_grads, jnp.zeros_like(kv_grads))
    wide_rows = activations.astype(jnp.float32)
    row_scale = lax.rsqrt(jnp.mean(wide_rows * wide_rows, axis=-1, keepdims=True) + norm_eps)
    normed = (wide_rows * row_scale * norm_gain).astype(jnp.bfloat16)
    partial = lax.dot_general(
        normed.reshape(tokens, features),
        kv_live.reshape(tokens, columns),
        (((0,), (0,)), ((), ())),
        preferred_element_type=jnp.float32,
    )
    partial = partial.astype(jnp.bfloat16).reshape(16, 2, 2, 64, columns)
    partial = partial.transpose(2, 1, 0, 3, 4)
    swapped = lax.all_to_all(partial, "core", 0, 0)
    halves = add_pair(swapped[0], swapped[1]).astype(jnp.bfloat16)
    swapped = lax.all_to_all(halves, "x_lo", 0, 0)
    quarters = add_pair(swapped[0], swapped[1]).astype(jnp.bfloat16)
    planes = lax.all_to_all(quarters, "z", 0, 0)
    weight_grad = jnp.sum(planes.astype(jnp.float32), axis=0)

    near = jnp.where(x_at == 0, own_quarter, x_quarter), jnp.where(x_at == 0, x_quarter, own_quarter)
    away = jnp.where(x_at == 0, core_quarter, far_quarter), jnp.where(x_at == 0, far_quarter, core_quarter)
    parts = [
        jnp.where(core_at == c, near[x], away[x]) for x in range(2) for c in range(2)
    ]
    slice_weights = jnp.stack(parts, 0).reshape(4, 8, 2, 64, columns)
    slice_weights = slice_weights.transpose(1, 2, 0, 3, 4).reshape(8, 512, columns)
    normed_grad = lax.dot_general(
        kv_all, slice_weights, (((0, 2), (0, 2)), ((), ())), preferred_element_type=jnp.float32
    ).reshape(batches, tok_rows, 512)
    offset = member * 512
    slice_gain = lax.dynamic_slice_in_dim(norm_gain, offset, 512, 0)
    slice_unit = (
        lax.dynamic_slice_in_dim(activations, offset, 512, 2).astype(jnp.float32) * row_scale
    )
    scaled = normed_grad * slice_gain
    inner = jnp.sum(scaled * slice_unit, axis=-1)
    inner = lax.all_to_all(jnp.broadcast_to(inner[None], (8,) + inner.shape), TENSOR, 0, 0)
    row_inner = jnp.sum(inner, axis=0)[:, :, None] / features
    input_grads = row_scale * (scaled - slice_unit * row_inner)
    input_grads = jnp.where(live_mask[:, :, None], input_grads, 0.0).astype(jnp.bfloat16)

    mean_grad = weight_grad / 64**0.5
    new_moment_one = beta_one * moment_one + (1.0 - beta_one) * mean_grad
    new_moment_two = beta_two * moment_two + (1.0 - beta_two) * mean_grad * mean_grad
    first_fixed = new_moment_one / (1.0 - beta_one**adam_step)
    second_fixed = new_moment_two / (1.0 - beta_two**adam_step)
    new_master = master - learn_rate * first_fixed / (jnp.sqrt(second_fixed) + adam_eps)
    return (input_grads, new_master, new_moment_one, new_moment_two)


def solution(mesh):
    fine = Mesh(mesh.devices.reshape(SIZES), TENSOR + DP)
    return jax.shard_map(
        on_device,
        mesh=fine,
        in_specs=(
            P(None, DP, None),
            P(None, DP, TENSOR),
            P(),
            P(DP, TENSOR),
            P(DP, TENSOR),
            P(DP, TENSOR),
            P(None, DP),
            P(None, DP),
        ),
        out_specs=(
            P(None, DP, TENSOR),
            P(DP, TENSOR),
            P(DP, TENSOR),
            P(DP, TENSOR),
        ),
        check_vma=False,
    )
```

time: 503 us -> 200 us (0.40)
  the two profiles are of different devices: /device:TPU:32 before, /device:TPU:2 now
where the time goes in v1:
time: 200 us
  blocking collectives  76.5 us (38%)
  waiting for transfers between devices  60 us (30%)
  starting transfers between devices  30.6 us (15%)
  between operations  14.2 us (7%)
  other arithmetic  9.92 us (5%)
  matrix products  5.61 us (3%)
  local copies, waits for them, and re-layouts  2.87 us (1%)
    all_to_all x1, blocking collectives, on_device(): planes = lax.all_to_all(quarters, 'z', 0, 0)  38.2 us
    all_to_all x1, waiting for transfers between devices, on_device(): own_quarter = lax.all_to_all(spread, 'z', 0, 0)  26.3 us
    all_gather x1, waiting for transfers between devices, on_device(): kv_all = lax.all_gather(kv_grads.reshape(tokens, columns), TENSOR, axis=0)  25.5 us
    all_to_all x1, starting transfers between devices, on_device(): own_quarter = lax.all_to_all(spread, 'z', 0, 0)  22.8 us
    all_to_all x1, blocking collectives, on_device(): swapped = lax.all_to_all(halves, 'x_lo', 0, 0)  20.8 us
    all_to_all x1, blocking collectives, on_device(): lax.all_to_all(jnp.broadcast_to(inner[None], (8,) + inner.shape), TENSOR,...  12.1 us
    ppermute x1, waiting for transfers between devices, on_device(): x_quarter = lax.ppermute(own_quarter, 'x_lo', SWAP)  6.12 us
    all_to_all x1, blocking collectives, on_device(): swapped = lax.all_to_all(partial, 'core', 0, 0)  5.42 us
  transfers between devices with their start and end apart: 6, of which 4 were waited for; matrix products, arithmetic and copies ran while one was open for 2% of the time, Pallas kernels for 0%

profile of v1, /device:TPU:2, one launch (start us, length us, event | category | flops | bytes accessed | tf_op | source)
XLA Modules:
  0.0 199.7 jit_solution(14687227048975036820)
XLA Ops:
  7.2 2.7 %fusion = f32[3,128]{1,0:T(4,128)S(1)} fusion(bf16[3,128,4096]{2,1,0:T(8,128)(2,1)} %param.8), kind=kLoop, calls=%fused_computation.2 | loop fusion | flops 4718208 | bytes 3147264 | tf_op jit(solution)/shard_map/reduce_sum | solution.py:54
  10.0 0.1 fusion.12
  10.0 2.6 %fusion.3 = bf16[4096,256]{1,0:T(8,128)(2,1)S(1)} fusion(bf16[3,128,4096]{2,1,0:T(8,128)(2,1)S(1)} %copy-done, f32[4096]{0:T(1024)} %param.10, f32[3,128]{1,0:T(4,128)S(1)} %add_rsqrt_fusion, bf16[3,128,256]{2,1,0:T(8,128)(2,1)} %param.9, pred[3,128]{1,0:T(4,128)(4,1)S(1)} %fusion.12), kind=kOutput, calls=%fused_computation.6 | convolution fusion | flops 812744704 | bytes 5457792 | tf_op jit(solution)/shard_map/dot_general | solution.py:56
  12.6 0.2 copy.26
  12.9 5.4 %all_to_all.25 = bf16[2,2,16,64,256]{4,3,1,2,0:T(8,128)(2,1)S(1)} all-to-all(bf16[2,2,16,64,256]{4,3,1,2,0:T(8,128)(2,1)S(1)} %bitcast.28), channel_id=1, replica_groups=mesh['x_hi'=2,'y'=4,'z'=16,'x_lo'=2,'core'=2] {'core'}, dimensions={0} | all-to-all | bytes 4194304 | tf_op jit(solution)/shard_map/all_to_all | solution.py:64
  18.3 0.4 fusion.7
  18.7 0.1 copy.22
  18.8 20.8 %all_to_all.26 = bf16[2,16,64,256]{3,2,1,0:T(8,128)(2,1)S(1)} all-to-all(bf16[2,16,64,256]{3,2,1,0:T(8,128)(2,1)S(1)} %copy.22), channel_id=1, replica_groups=mesh['x_hi'=2,'y'=4,'z'=16,'x_lo'=2,'core'=2] {'x_lo'}, dimensions={0} | all-to-all | bytes 2097152 | tf_op jit(solution)/shard_map/all_to_all | solution.py:66
  39.6 0.2 fusion.8
  39.8 38.2 %all_to_all.27 = bf16[16,64,256]{2,1,0:T(8,128)(2,1)S(1)} all-to-all(bf16[16,64,256]{2,1,0:T(8,128)(2,1)S(1)} %fusion.8), channel_id=1, replica_groups=mesh['x_hi'=2,'y'=4,'z'=16,'x_lo'=2,'core'=2] {'z'}, dimensions={0} | all-to-all | bytes 1048576 | tf_op jit(solution)/shard_map/all_to_all | solution.py:68
  78.0 0.1 convert_reduce_fusion
  78.1 0.7 divide_subtract_fusion
  78.8 0.7 collective-permute-start
  79.5 0.8 broadcast_in_dim.23
  80.3 22.8 %all-to-all-start = ((bf16[16,64,256]{2,1,0:T(8,128)(2,1)}), bf16[16,64,256]{2,1,0:T(8,128)(2,1)}, u32[]{:S(2)}, u32[]{:S(2)}) async-start(bf16[16,64,256]{2,1,0:T(8,128)(2,1)} %broadcast_in_dim.23), calls=%async_computation | async-start | bytes 1048576 | tf_op jit(solution)/shard_map/all_to_all | solution.py:44
  103.1 0.0 all-gather.2.cloned.1.call-start
  103.2 0.7 all-gather.2.cloned.1.call-update
  103.8 26.3 %all-to-all-done = bf16[16,64,256]{2,1,0:T(8,128)(2,1)} async-done(((bf16[16,64,256]{2,1,0:T(8,128)(2,1)}), bf16[16,64,256]{2,1,0:T(8,128)(2,1)}, u32[]{:S(2)}, u32[]{:S(2)}) %all-to-all-start) | async-done | bytes 524320 | tf_op jit(solution)/shard_map/all_to_all | solution.py:44
  130.1 3.3 %collective-permute-start.1 = (bf16[16,64,256]{2,1,0:T(8,128)(2,1)}, bf16[16,64,256]{2,1,0:T(8,128)(2,1)}, u32[]{:S(2)}, u32[]{:S(2)}) collective-permute-start(bf16[16,64,256]{2,1,0:T(8,128)(2,1)} %all-to-all-done), channel_id=1, source_target_pairs={{0,2},{2,0},{1,3},{3,1},{4,6},{6,4},{5,7},{7,5},{8,10},{10,8},{9,1... | collective-permute-start | bytes 1572872 | tf_op jit(solution)/shard_map/ppermute | solution.py:45
  133.4 1.9 collective-permute-start.2
  135.4 6.1 %collective-permute-done.1 = bf16[16,64,256]{2,1,0:T(8,128)(2,1)} collective-permute-done((bf16[16,64,256]{2,1,0:T(8,128)(2,1)}, bf16[16,64,256]{2,1,0:T(8,128)(2,1)}, u32[]{:S(2)}, u32[]{:S(2)}) %collective-permute-start.1) | collective-permute-done | bytes 524320 | tf_op jit(solution)/shard_map/ppermute | solution.py:45
  141.5 1.9 collective-permute-start.3
  143.4 0.8 dynamic_slice.6
  144.2 1.4 collective-permute-done.3
  145.6 1.7 broadcast_select_fusion.7
  147.3 1.6 pad_maximum_fusion
  148.9 25.5 %all-gather.2.cloned.1.call-done = bf16[8,384,256]{2,1,0:T(8,128)(2,1)} async-done(((bf16[1,384,256]{2,1,0:T(8,128)(2,1)}), bf16[8,384,256]{2,1,0:T(8,128)(2,1)}) %all-gather.2.cloned.1.call-update) | async-done | bytes 1572880 | tf_op jit(solution)/shard_map/all_gather | solution.py:48
  174.4 3.0 %fusion.14 = f32[512,384,1]{0,1,2:T(8,128)S(1)} fusion(bf16[8,512,256]{2,1,0:T(8,128)(2,1)} %bitcast.31, bf16[8,384,256]{2,1,0:T(8,128)(2,1)} %all-gather.2.cloned.1.call-done), kind=kOutput, calls=%fused_computation.38 | convolution fusion | flops 805306368 | bytes 4456448 | tf_op jit(solution)/shard_map/dot_general | solution.py:78
  177.5 0.9 copy-done.1
  178.3 0.3 multiply_reduce_fusion
  178.6 12.1 %all_to_all.28 = f32[8,3,128]{2,1,0:T(4,128)S(1)} all-to-all(f32[8,3,128]{2,1,0:T(4,128)S(1)} %broadcast_in_dim.24), channel_id=1, replica_groups=mesh['x_hi'=2,'y'=4,'z'=16,'x_lo'=2,'core'=2] {'x_hi','y'}, dimensions={0} | all-to-all | bytes 24576 | tf_op jit(solution)/shard_map/all_to_all | solution.py:88
  190.7 2.2 %select_convert_fusion = bf16[3,128,512]{2,1,0:T(8,128)(2,1)} fusion(f32[3,128,512]{2,1,0:T(8,128)} %bitcast.30, f32[3,128]{1,0:T(4,128)S(1)} %broadcast_multiply_fusion, f32[512]{0:T(512)S(1)} %dynamic_slice.6, f32[3,128]{1,0:T(4,128)S(1)} %add_rsqrt_fusion, pred[3,128]{1,0:T(4,128)(4,1)S(1)} %fusion.12, bf16[3,128,4096]{2,1,0:T(8,128)(2,1)S(1)} %copy-done, ...), kind=kLoop, calls=%fused_computation.15 | loop fusion | flops 1572864 | bytes 1578372 | tf_op jit(solution)/shard_map/convert_element_type | solution.py:91
  (19 shorter events, 0.1 us)
Async XLA Ops:
  7.2 2.9 %copy-start = (bf16[3,128,4096]{2,1,0:T(8,128)(2,1)S(1)}, bf16[3,128,4096]{2,1,0:T(8,128)(2,1)}, u32[]{:S(2)}) copy-start(bf16[3,128,4096]{2,1,0:T(8,128)(2,1)} %param.8) | copy-start | bytes 9437188
  7.2 2.8 %copy-start.6 = (s32[3,1]{0,1:T(1,128)S(1)}, s32[3,1]{0,1:T(1,128)}, u32[]{:S(2)}) copy-start(s32[3,1]{0,1:T(1,128)} %param.14) | copy-start | bytes 40
  7.2 2.8 %copy-start.5 = (s32[3,128]{1,0:T(4,128)S(1)}, s32[3,128]{1,0:T(4,128)}, u32[]{:S(2)}) copy-start(s32[3,128]{1,0:T(4,128)} %param.15) | copy-start | bytes 4612
  39.6 38.5 %copy-start.2 = (f32[64,256]{1,0:T(8,128)S(1)}, f32[64,256]{1,0:T(8,128)}, u32[]{:S(2)}) copy-start(f32[64,256]{1,0:T(8,128)} %param.11) | copy-start | bytes 196612
  39.6 38.5 %copy-start.3 = (f32[64,256]{1,0:T(8,128)S(1)}, f32[64,256]{1,0:T(8,128)}, u32[]{:S(2)}) copy-start(f32[64,256]{1,0:T(8,128)} %param.12) | copy-start | bytes 196612
  39.6 38.5 %copy-start.4 = (f32[64,256]{1,0:T(8,128)S(1)}, f32[64,256]{1,0:T(8,128)}, u32[]{:S(2)}) copy-start(f32[64,256]{1,0:T(8,128)} %param.13) | copy-start | bytes 196612
  78.8 0.7 collective-permute-start
  80.3 49.7 %all-to-all-start = ((bf16[16,64,256]{2,1,0:T(8,128)(2,1)}), bf16[16,64,256]{2,1,0:T(8,128)(2,1)}, u32[]{:S(2)}, u32[]{:S(2)}) async-start(bf16[16,64,256]{2,1,0:T(8,128)(2,1)} %broadcast_in_dim.23), calls=%async_computation | async-start | bytes 1048576 | tf_op jit(solution)/shard_map/all_to_all | solution.py:44
  103.1 71.3 %all-gather.2.cloned.1.call-start = ((), (), s32[]{:S(2)}) async-start(), calls=%async_computation.5 | async-start | bytes 1769472 | tf_op jit(solution)/shard_map/all_gather | solution.py:48
  130.1 11.4 %collective-permute-start.1 = (bf16[16,64,256]{2,1,0:T(8,128)(2,1)}, bf16[16,64,256]{2,1,0:T(8,128)(2,1)}, u32[]{:S(2)}, u32[]{:S(2)}) collective-permute-start(bf16[16,64,256]{2,1,0:T(8,128)(2,1)} %all-to-all-done), channel_id=1, source_target_pairs={{0,2},{2,0},{1,3},{3,1},{4,6},{6,4},{5,7},{7,5},{8,10},{10,8},{9,1... | collective-permute-start | bytes 1572872 | tf_op jit(solution)/shard_map/ppermute | solution.py:45
  133.4 10.7 %collective-permute-start.2 = (bf16[16,64,256]{2,1,0:T(8,128)(2,1)}, bf16[16,64,256]{2,1,0:T(8,128)(2,1)}, u32[]{:S(2)}, u32[]{:S(2)}) collective-permute-start(bf16[16,64,256]{2,1,0:T(8,128)(2,1)} %all-to-all-done), channel_id=1, source_target_pairs={{0,1},{1,0},{2,3},{3,2},{4,5},{5,4},{6,7},{7,6},{8,9},{9,8},{10,11... | collective-permute-start | bytes 1572872 | tf_op jit(solution)/shard_map/ppermute | solution.py:46
  141.5 4.1 %collective-permute-start.3 = (bf16[16,64,256]{2,1,0:T(8,128)(2,1)}, bf16[16,64,256]{2,1,0:T(8,128)(2,1)}, u32[]{:S(2)}, u32[]{:S(2)}) collective-permute-start(bf16[16,64,256]{2,1,0:T(8,128)(2,1)} %collective-permute-done.1), channel_id=1, source_target_pairs={{0,1},{1,0},{2,3},{3,2},{4,5},{5,4},{6,7},{7,6},{8,9},{9,8},{10,11... | collective-permute-start | bytes 1572872 | tf_op jit(solution)/shard_map/ppermute | solution.py:47
  177.5 0.9 copy-start.1
Sparse Core Ops, SparseCore 0:
  107.1 67.2 all-gather.1

commit v2 on v1

--- a/solution.py
+++ b/solution.py
@@ -40,12 +40,7 @@
     member = lax.axis_index(TENSOR)
 
     moved = lax.ppermute(master.astype(jnp.bfloat16), TENSOR + DP, slice_owner_pairs())
-    spread = jnp.broadcast_to(moved[None], (16,) + moved.shape)
-    own_quarter = lax.all_to_all(spread, "z", 0, 0)
-    x_quarter = lax.ppermute(own_quarter, "x_lo", SWAP)
-    core_quarter = lax.ppermute(own_quarter, "core", SWAP)
-    far_quarter = lax.ppermute(x_quarter, "core", SWAP)
-    kv_all = lax.all_gather(kv_grads.reshape(tokens, columns), TENSOR, axis=0)
+    flat_kv = kv_grads.reshape(tokens, columns)
 
     position = lax.broadcasted_iota(jnp.int32, (batches, tok_rows), 1)
     live_mask = (position < lengths) & (labels != -100)
@@ -63,10 +58,18 @@
     partial = partial.transpose(2, 1, 0, 3, 4)
     swapped = lax.all_to_all(partial, "core", 0, 0)
     halves = add_pair(swapped[0], swapped[1]).astype(jnp.bfloat16)
-    swapped = lax.all_to_all(halves, "x_lo", 0, 0)
-    quarters = add_pair(swapped[0], swapped[1]).astype(jnp.bfloat16)
+    keep = jnp.where(x_at == 0, halves[0], halves[1])
+    give = jnp.where(x_at == 0, halves[1], halves[0])
+    give, keep, moved, flat_kv = lax.optimization_barrier((give, keep, moved, flat_kv))
+    arrived = lax.ppermute(give, "x_lo", SWAP)
+    kv_all = lax.all_to_all(jnp.broadcast_to(flat_kv[None], (8,) + flat_kv.shape), TENSOR, 0, 0)
+    own_quarter = lax.all_gather(moved, "z", axis=0)
+    arrived, own_quarter, kv_all = lax.optimization_barrier((arrived, own_quarter, kv_all))
+    x_quarter = lax.ppermute(own_quarter, "x_lo", SWAP)
+    core_quarter = lax.ppermute(own_quarter, "core", SWAP)
+    quarters = add_pair(keep, arrived).astype(jnp.bfloat16)
     planes = lax.all_to_all(quarters, "z", 0, 0)
-    weight_grad = jnp.sum(planes.astype(jnp.float32), axis=0)
+    far_quarter = lax.ppermute(x_quarter, "core", SWAP)
 
     near = jnp.where(x_at == 0, own_quarter, x_quarter), jnp.where(x_at == 0, x_quarter, own_quarter)
     away = jnp.where(x_at == 0, core_quarter, far_quarter), jnp.where(x_at == 0, far_quarter, core_quarter)
@@ -85,7 +88,9 @@
     )
     scaled = normed_grad * slice_gain
     inner = jnp.sum(scaled * slice_unit, axis=-1)
+    inner, planes = lax.optimization_barrier((inner, planes))
     inner = lax.all_to_all(jnp.broadcast_to(inner[None], (8,) + inner.shape), TENSOR, 0, 0)
+    weight_grad = jnp.sum(planes.astype(jnp.float32), axis=0)
     row_inner = jnp.sum(inner, axis=0)[:, :, None] / features
     input_grads = row_scale * (scaled - slice_unit * row_inner)
     input_grads = jnp.where(live_mask[:, :, None], input_grads, 0.0).astype(jnp.bfloat16)

time: 200 us -> 123 us (0.61)
  the two profiles are of different devices: /device:TPU:2 before, /device:TPU:32 now
where the time goes in v2:
time: 123 us; the launch traced here: 122 us
  starting transfers between devices  50.3 us (41%)
  blocking collectives  30.1 us (24%)
  waiting for transfers between devices  22.1 us (18%)
  other arithmetic  10.3 us (8%)
  matrix products  4.85 us (4%)
  local copies, waits for them, and re-layouts  3.48 us (3%)
    all_gather x1, blocking collectives, on_device(): own_quarter = lax.all_gather(moved, 'z', axis=0)  30.1 us
    all_to_all x1, starting transfers between devices, on_device(): lax.all_to_all(jnp.broadcast_to(flat_kv[None], (8,) + flat_kv.shape), TEN...  18.4 us
    all_to_all x1, starting transfers between devices, on_device(): planes = lax.all_to_all(quarters, 'z', 0, 0)  9.91 us
    all_to_all x1, starting transfers between devices, on_device(): lax.all_to_all(jnp.broadcast_to(inner[None], (8,) + inner.shape), TENSOR,...  7.92 us
    all_to_all x1, waiting for transfers between devices, on_device(): lax.all_to_all(jnp.broadcast_to(inner[None], (8,) + inner.shape), TENSOR,...  6.92 us
    ppermute x1, waiting for transfers between devices, on_device(): x_quarter = lax.ppermute(own_quarter, 'x_lo', SWAP)  6.7 us
    all_to_all x1, starting transfers between devices, on_device(): swapped = lax.all_to_all(partial, 'core', 0, 0)  3.76 us
    all_to_all x1, waiting for transfers between devices, on_device(): planes = lax.all_to_all(quarters, 'z', 0, 0)  3.71 us
  transfers between devices with their start and end apart: 9, of which 5 were waited for; matrix products, arithmetic and copies ran while one was open for 10% of the time, Pallas kernels for 0%

profile of v2, /device:TPU:32, one launch (start us, length us, event | category | flops | bytes accessed | tf_op | source)
XLA Modules:
  0.0 122.0 jit_solution(12894193951029371902)
XLA Ops:
  0.7 1.0 convert_element_type.48
  1.7 0.7 collective-permute-start
  2.3 2.6 %fusion = f32[3,128]{1,0:T(4,128)S(1)} fusion(bf16[3,128,4096]{2,1,0:T(8,128)(2,1)} %param.8), kind=kLoop, calls=%fused_computation.2 | loop fusion | flops 4718208 | bytes 3147264 | tf_op jit(solution)/shard_map/reduce_sum | solution.py:49
  4.9 0.1 fusion.13
  5.0 2.7 %fusion.3 = bf16[4096,256]{1,0:T(8,128)(2,1)S(1)} fusion(bf16[3,128,4096]{2,1,0:T(8,128)(2,1)S(1)} %copy-done, f32[4096]{0:T(1024)S(1)} %copy-done.7, f32[3,128]{1,0:T(4,128)S(1)} %add_rsqrt_fusion, bf16[3,128,256]{2,1,0:T(8,128)(2,1)} %param.9, pred[3,128]{1,0:T(4,128)(4,1)S(1)} %fusion.13), kind=kOutput, calls=%fused_computation.6 | convolution fusion | flops 812744704 | bytes 5457792 | tf_op jit(solution)/shard_map/dot_general | solution.py:51
  7.7 1.5 %copy.56 = bf16[16,2,2,64,256]{4,3,1,0,2:T(8,128)(2,1)} copy(bf16[16,2,2,64,256]{4,3,2,1,0:T(8,128)(2,1)S(1)} %bitcast.55) | data formatting | bytes 4194304 | tf_op jit(solution)/shard_map/reshape | solution.py:57
  9.2 3.8 %all-to-all-start = ((bf16[2,2,16,64,256]{4,3,1,2,0:T(8,128)(2,1)}), bf16[2,2,16,64,256]{4,3,1,2,0:T(8,128)(2,1)S(1)}, u32[]{:S(2)}, u32[]{:S(2)}) async-start(bf16[2,2,16,64,256]{4,3,1,2,0:T(8,128)(2,1)} %bitcast.50), calls=%async_computation | async-start | bytes 4194304 | tf_op jit(solution)/shard_map/all_to_all | solution.py:59
  13.0 2.8 %all-to-all-done = bf16[2,2,16,64,256]{4,3,1,2,0:T(8,128)(2,1)S(1)} async-done(((bf16[2,2,16,64,256]{4,3,1,2,0:T(8,128)(2,1)}), bf16[2,2,16,64,256]{4,3,1,2,0:T(8,128)(2,1)S(1)}, u32[]{:S(2)}, u32[]{:S(2)}) %all-to-all-start) | async-done | bytes 2097184 | tf_op jit(solution)/shard_map/all_to_all | solution.py:59
  15.8 0.4 add_convert_fusion
  16.2 0.9 fusion.9
  17.1 1.3 %broadcast_in_dim.44 = bf16[8,384,256]{2,1,0:T(8,128)(2,1)} broadcast(bf16[384,256]{1,0:T(8,128)(2,1)S(1)} %bitcast.61), dimensions={1,2} | broadcast | bytes 1769472 | tf_op jit(solution)/shard_map/broadcast_in_dim | solution.py:65
  18.4 18.4 %all-to-all-start.1 = ((bf16[8,384,256]{2,1,0:T(8,128)(2,1)}), bf16[8,384,256]{2,1,0:T(8,128)(2,1)S(1)}, u32[]{:S(2)}, u32[]{:S(2)}) async-start(bf16[8,384,256]{2,1,0:T(8,128)(2,1)} %broadcast_in_dim.44), calls=%async_computation.1 | async-start | bytes 3145728 | tf_op jit(solution)/shard_map/all_to_all | solution.py:65
  36.8 3.4 %collective-permute-start.1 = (bf16[16,64,256]{2,1,0:T(8,128)(2,1)}, bf16[16,64,256]{2,1,0:T(8,128)(2,1)S(1)}, u32[]{:S(2)}, u32[]{:S(2)}) collective-permute-start(bf16[16,64,256]{2,1,0:T(8,128)(2,1)} %fusion.9), channel_id=1, source_target_pairs={{0,2},{2,0},{1,3},{3,1},{4,6},{6,4},{5,7},{7,5},{8,10},{10,8},{9,1... | collective-permute-start | bytes 1572872 | tf_op jit(solution)/shard_map/ppermute | solution.py:64
  40.2 30.1 %all-gather = bf16[1024,256]{1,0:T(8,128)(2,1)S(1)} all-gather(bf16[64,256]{1,0:T(8,128)(2,1)S(1)} %collective-permute-done), channel_id=2, replica_groups=mesh['x_hi'=2,'y'=4,'z'=16,'x_lo'=2,'core'=2] {'z'}, dimensions={0}, use_global_device_ids=true | all-gather | bytes 557056 | tf_op jit(solution)/shard_map/all_gather | solution.py:66
  70.3 1.0 add_convert_fusion.1
  71.3 9.9 %all-to-all-start.2 = ((bf16[16,64,256]{2,1,0:T(8,128)(2,1)}), bf16[16,64,256]{2,1,0:T(8,128)(2,1)S(1)}, u32[]{:S(2)}, u32[]{:S(2)}) async-start(bf16[16,64,256]{2,1,0:T(8,128)(2,1)} %add_convert_fusion.1), calls=%async_computation.2 | async-start | bytes 1048576 | tf_op jit(solution)/shard_map/all_to_all | solution.py:71
  81.2 2.4 %collective-permute-start.2 = (bf16[16,64,256]{2,1,0:T(8,128)(2,1)S(1)}, bf16[16,64,256]{2,1,0:T(8,128)(2,1)S(1)}, u32[]{:S(2)}, u32[]{:S(2)}) collective-permute-start(bf16[16,64,256]{2,1,0:T(8,128)(2,1)S(1)} %bitcast.51), channel_id=1, source_target_pairs={{0,2},{2,0},{1,3},{3,1},{4,6},{6,4},{5,7},{7,5},{8,10},{10,8},{9,1... | collective-permute-start | bytes 1572872 | tf_op jit(solution)/shard_map/ppermute | solution.py:68
  83.6 1.9 %collective-permute-start.3 = (bf16[16,64,256]{2,1,0:T(8,128)(2,1)S(1)}, bf16[16,64,256]{2,1,0:T(8,128)(2,1)}, u32[]{:S(2)}, u32[]{:S(2)}) collective-permute-start(bf16[16,64,256]{2,1,0:T(8,128)(2,1)S(1)} %bitcast.52), channel_id=1, source_target_pairs={{0,1},{1,0},{2,3},{3,2},{4,5},{5,4},{6,7},{7,6},{8,9},{9,8},{10,11... | collective-permute-start | bytes 1572872 | tf_op jit(solution)/shard_map/ppermute | solution.py:69
  85.5 6.7 %collective-permute-done.2 = bf16[16,64,256]{2,1,0:T(8,128)(2,1)S(1)} collective-permute-done((bf16[16,64,256]{2,1,0:T(8,128)(2,1)S(1)}, bf16[16,64,256]{2,1,0:T(8,128)(2,1)S(1)}, u32[]{:S(2)}, u32[]{:S(2)}) %collective-permute-start.2) | collective-permute-done | bytes 524320 | tf_op jit(solution)/shard_map/ppermute | solution.py:68
  92.2 1.9 %collective-permute-start.4 = (bf16[16,64,256]{2,1,0:T(8,128)(2,1)S(1)}, bf16[16,64,256]{2,1,0:T(8,128)(2,1)}, u32[]{:S(2)}, u32[]{:S(2)}) collective-permute-start(bf16[16,64,256]{2,1,0:T(8,128)(2,1)S(1)} %collective-permute-done.2), channel_id=1, source_target_pairs={{0,1},{1,0},{2,3},{3,2},{4,5},{5,4},{6,7},{7,6},{8,9},{9,8},{10,11... | collective-permute-start | bytes 1572872 | tf_op jit(solution)/shard_map/ppermute | solution.py:72
  94.2 0.1 dynamic_slice.6
  94.3 1.9 %collective-permute-done.4 = bf16[16,64,256]{2,1,0:T(8,128)(2,1)} collective-permute-done((bf16[16,64,256]{2,1,0:T(8,128)(2,1)S(1)}, bf16[16,64,256]{2,1,0:T(8,128)(2,1)}, u32[]{:S(2)}, u32[]{:S(2)}) %collective-permute-start.4) | collective-permute-done | bytes 524320 | tf_op jit(solution)/shard_map/ppermute | solution.py:72
  96.2 1.4 %broadcast_select_fusion.7 = (bf16[16,64,256]{2,1,0:T(8,128)(2,1)S(1)}, bf16[16,64,256]{2,1,0:T(8,128)(2,1)S(1)}, bf16[16,64,256]{2,1,0:T(8,128)(2,1)S(1)}, bf16[16,64,256]{2,1,0:T(8,128)(2,1)S(1)}) fusion(pred[]{:T(512)S(6)} %eq.7, bf16[16,64,256]{2,1,0:T(8,128)(2,1)S(1)} %bitcast.53, bf16[16,64,256]{2,1,0:T(8,128)(2,1)S(1)} %collective-permute-done.2, ...), kind=kLoop, calls=%fused_computation.30 | loop fusion | flops 2097152 | bytes 4194307 | tf_op jit(solution)/shard_map/jit(_where)/select_n | solution.py:77
  97.5 0.3 pad_maximum_fusion
  97.8 2.2 %multiply_reduce_fusion = (f32[3,128]{1,0:T(4,128)S(1)}, f32[3,128,512]{2,1,0:T(8,128)S(1)}) fusion(f32[3,128]{1,0:T(4,128)S(1)} %add_rsqrt_fusion, bf16[3,128,4096]{2,1,0:T(8,128)(2,1)} %param.8, s32[]{:T(128)S(6)} %select_n.87, f32[512]{0:T(512)S(1)} %dynamic_slice.6, bf16[3,128,8,256]{3,1,0,2:T(8,128)(2,1)S(1)} %bitcast.60, ...), kind=kOutput, calls=%fused_computation.18 | convolution fusion | flops 806289024 | bytes 4854788 | tf_op jit(solution)/shard_map/dot_general | solution.py:81
  100.0 3.7 %all-to-all-done.2 = bf16[16,64,256]{2,1,0:T(8,128)(2,1)S(1)} async-done(((bf16[16,64,256]{2,1,0:T(8,128)(2,1)}), bf16[16,64,256]{2,1,0:T(8,128)(2,1)S(1)}, u32[]{:S(2)}, u32[]{:S(2)}) %all-to-all-start.2) | async-done | bytes 524320 | tf_op jit(solution)/shard_map/all_to_all | solution.py:71
  103.7 0.6 broadcast_in_dim.45
  104.3 7.9 %all-to-all-start.3 = ((f32[8,3,128]{2,1,0:T(4,128)}), f32[8,3,128]{2,1,0:T(4,128)S(1)}, u32[]{:S(2)}, u32[]{:S(2)}) async-start(f32[8,3,128]{2,1,0:T(4,128)} %broadcast_in_dim.45), calls=%async_computation.3 | async-start | bytes 32768 | tf_op jit(solution)/shard_map/all_to_all | solution.py:92
  112.2 0.1 convert_reduce_fusion
  112.3 0.7 divide_subtract_fusion
  113.0 6.9 %all-to-all-done.3 = f32[8,3,128]{2,1,0:T(4,128)S(1)} async-done(((f32[8,3,128]{2,1,0:T(4,128)}), f32[8,3,128]{2,1,0:T(4,128)S(1)}, u32[]{:S(2)}, u32[]{:S(2)}) %all-to-all-start.3) | async-done | bytes 12320 | tf_op jit(solution)/shard_map/all_to_all | solution.py:92
  120.0 2.0 %select_convert_fusion = bf16[3,128,512]{2,1,0:T(8,128)(2,1)} fusion(f32[3,128,512]{2,1,0:T(8,128)S(1)} %get-tuple-element.30, f32[3,128]{1,0:T(4,128)S(1)} %broadcast_multiply_fusion, f32[3,128]{1,0:T(4,128)S(1)} %add_rsqrt_fusion, pred[3,128]{1,0:T(4,128)(4,1)S(1)} %fusion.13, bf16[3,128,4096]{2,1,0:T(8,128)(2,1)} %param.8, s32[]{:T(128)S(6)} %select_n.87), kind=kLoop, calls=%fused_computation.17 | loop fusion | flops 1376256 | bytes 1576324 | tf_op jit(solution)/shard_map/convert_element_type | solution.py:96
  (24 shorter events, 0.1 us)
Async XLA Ops:
  0.6 4.4 %copy-start = (bf16[3,128,4096]{2,1,0:T(8,128)(2,1)S(1)}, bf16[3,128,4096]{2,1,0:T(8,128)(2,1)}, u32[]{:S(2)}) copy-start(bf16[3,128,4096]{2,1,0:T(8,128)(2,1)} %param.8) | copy-start | bytes 9437188
  0.6 4.3 %copy-start.5 = (s32[3,128]{1,0:T(4,128)S(1)}, s32[3,128]{1,0:T(4,128)}, u32[]{:S(2)}) copy-start(s32[3,128]{1,0:T(4,128)} %param.15) | copy-start | bytes 4612
  0.7 4.3 %copy-start.6 = (s32[3,1]{0,1:T(1,128)S(1)}, s32[3,1]{0,1:T(1,128)}, u32[]{:S(2)}) copy-start(s32[3,1]{0,1:T(1,128)} %param.14) | copy-start | bytes 40
  0.7 4.4 %copy-start.7 = (f32[4096]{0:T(1024)S(1)}, f32[4096]{0:T(1024)}, u32[]{:S(2)}) copy-start(f32[4096]{0:T(1024)} %param.10) | copy-start | bytes 49156
  1.7 15.5 %collective-permute-start = (bf16[64,256]{1,0:T(8,128)(2,1)S(1)}, bf16[64,256]{1,0:T(8,128)(2,1)S(1)}, u32[]{:S(2)}, u32[]{:S(2)}) collective-permute-start(bf16[64,256]{1,0:T(8,128)(2,1)S(1)} %convert_element_type.48), channel_id=1, source_target_pairs={{0,0},{1,1},{2,2},{3,3},{4,4},{5,5},{6,6},{7,7},{8,64},{9,65},{10,... | collective-permute-start | bytes 98312 | tf_op jit(solution)/shard_map/ppermute | solution.py:42
  9.2 6.6 %all-to-all-start = ((bf16[2,2,16,64,256]{4,3,1,2,0:T(8,128)(2,1)}), bf16[2,2,16,64,256]{4,3,1,2,0:T(8,128)(2,1)S(1)}, u32[]{:S(2)}, u32[]{:S(2)}) async-start(bf16[2,2,16,64,256]{4,3,1,2,0:T(8,128)(2,1)} %bitcast.50), calls=%async_computation | async-start | bytes 4194304 | tf_op jit(solution)/shard_map/all_to_all | solution.py:59
  16.2 1.0 copy-start.2
  18.4 51.9 %all-to-all-start.1 = ((bf16[8,384,256]{2,1,0:T(8,128)(2,1)}), bf16[8,384,256]{2,1,0:T(8,128)(2,1)S(1)}, u32[]{:S(2)}, u32[]{:S(2)}) async-start(bf16[8,384,256]{2,1,0:T(8,128)(2,1)} %broadcast_in_dim.44), calls=%async_computation.1 | async-start | bytes 3145728 | tf_op jit(solution)/shard_map/all_to_all | solution.py:65
  36.8 33.5 %collective-permute-start.1 = (bf16[16,64,256]{2,1,0:T(8,128)(2,1)}, bf16[16,64,256]{2,1,0:T(8,128)(2,1)S(1)}, u32[]{:S(2)}, u32[]{:S(2)}) collective-permute-start(bf16[16,64,256]{2,1,0:T(8,128)(2,1)} %fusion.9), channel_id=1, source_target_pairs={{0,2},{2,0},{1,3},{3,1},{4,6},{6,4},{5,7},{7,5},{8,10},{10,8},{9,1... | collective-permute-start | bytes 1572872 | tf_op jit(solution)/shard_map/ppermute | solution.py:64
  71.3 32.4 %all-to-all-start.2 = ((bf16[16,64,256]{2,1,0:T(8,128)(2,1)}), bf16[16,64,256]{2,1,0:T(8,128)(2,1)S(1)}, u32[]{:S(2)}, u32[]{:S(2)}) async-start(bf16[16,64,256]{2,1,0:T(8,128)(2,1)} %add_convert_fusion.1), calls=%async_computation.2 | async-start | bytes 1048576 | tf_op jit(solution)/shard_map/all_to_all | solution.py:71
  81.2 11.1 %collective-permute-start.2 = (bf16[16,64,256]{2,1,0:T(8,128)(2,1)S(1)}, bf16[16,64,256]{2,1,0:T(8,128)(2,1)S(1)}, u32[]{:S(2)}, u32[]{:S(2)}) collective-permute-start(bf16[16,64,256]{2,1,0:T(8,128)(2,1)S(1)} %bitcast.51), channel_id=1, source_target_pairs={{0,2},{2,0},{1,3},{3,1},{4,6},{6,4},{5,7},{7,5},{8,10},{10,8},{9,1... | collective-permute-start | bytes 1572872 | tf_op jit(solution)/shard_map/ppermute | solution.py:68
  83.6 10.6 %collective-permute-start.3 = (bf16[16,64,256]{2,1,0:T(8,128)(2,1)S(1)}, bf16[16,64,256]{2,1,0:T(8,128)(2,1)}, u32[]{:S(2)}, u32[]{:S(2)}) collective-permute-start(bf16[16,64,256]{2,1,0:T(8,128)(2,1)S(1)} %bitcast.52), channel_id=1, source_target_pairs={{0,1},{1,0},{2,3},{3,2},{4,5},{5,4},{6,7},{7,6},{8,9},{9,8},{10,11... | collective-permute-start | bytes 1572872 | tf_op jit(solution)/shard_map/ppermute | solution.py:69
  92.2 3.9 %collective-permute-start.4 = (bf16[16,64,256]{2,1,0:T(8,128)(2,1)S(1)}, bf16[16,64,256]{2,1,0:T(8,128)(2,1)}, u32[]{:S(2)}, u32[]{:S(2)}) collective-permute-start(bf16[16,64,256]{2,1,0:T(8,128)(2,1)S(1)} %collective-permute-done.2), channel_id=1, source_target_pairs={{0,1},{1,0},{2,3},{3,2},{4,5},{5,4},{6,7},{7,6},{8,9},{9,8},{10,11... | collective-permute-start | bytes 1572872 | tf_op jit(solution)/shard_map/ppermute | solution.py:72
  97.8 14.5 %copy-start.1 = (f32[64,256]{1,0:T(8,128)S(1)}, f32[64,256]{1,0:T(8,128)}, u32[]{:S(2)}) copy-start(f32[64,256]{1,0:T(8,128)} %param.11) | copy-start | bytes 196612
  97.8 14.5 %copy-start.3 = (f32[64,256]{1,0:T(8,128)S(1)}, f32[64,256]{1,0:T(8,128)}, u32[]{:S(2)}) copy-start(f32[64,256]{1,0:T(8,128)} %param.12) | copy-start | bytes 196612
  97.8 14.5 %copy-start.4 = (f32[64,256]{1,0:T(8,128)S(1)}, f32[64,256]{1,0:T(8,128)}, u32[]{:S(2)}) copy-start(f32[64,256]{1,0:T(8,128)} %param.13) | copy-start | bytes 196612
  104.3 15.6 %all-to-all-start.3 = ((f32[8,3,128]{2,1,0:T(4,128)}), f32[8,3,128]{2,1,0:T(4,128)S(1)}, u32[]{:S(2)}, u32[]{:S(2)}) async-start(f32[8,3,128]{2,1,0:T(4,128)} %broadcast_in_dim.45), calls=%async_computation.3 | async-start | bytes 32768 | tf_op jit(solution)/shard_map/all_to_all | solution.py:92

commit v3 on v2

--- a/solution.py
+++ b/solution.py
@@ -39,8 +39,10 @@
     x_at, core_at = lax.axis_index("x_lo"), lax.axis_index("core")
     member = lax.axis_index(TENSOR)
 
-    moved = lax.ppermute(master.astype(jnp.bfloat16), TENSOR + DP, slice_owner_pairs())
+    moved = lax.ppermute(master, TENSOR + DP, slice_owner_pairs()).astype(jnp.bfloat16)
     flat_kv = kv_grads.reshape(tokens, columns)
+    kv_spread = jnp.broadcast_to(flat_kv[None], (8,) + flat_kv.shape)
+    activations, kv_spread = lax.optimization_barrier((activations, kv_spread))
 
     position = lax.broadcasted_iota(jnp.int32, (batches, tok_rows), 1)
     live_mask = (position < lengths) & (labels != -100)
@@ -56,19 +58,23 @@
     )
     partial = partial.astype(jnp.bfloat16).reshape(16, 2, 2, 64, columns)
     partial = partial.transpose(2, 1, 0, 3, 4)
-    swapped = lax.all_to_all(partial, "core", 0, 0)
-    halves = add_pair(swapped[0], swapped[1]).astype(jnp.bfloat16)
+    give = jnp.where(core_at == 0, partial[1], partial[0])
+    keep = jnp.where(core_at == 0, partial[0], partial[1])
+    give, keep, moved = lax.optimization_barrier((give, keep, moved))
+    arrived = lax.ppermute(give, "core", SWAP)
+    halves = add_pair(keep, arrived).astype(jnp.bfloat16)
     keep = jnp.where(x_at == 0, halves[0], halves[1])
     give = jnp.where(x_at == 0, halves[1], halves[0])
-    give, keep, moved, flat_kv = lax.optimization_barrier((give, keep, moved, flat_kv))
+    give, keep, moved, kv_spread = lax.optimization_barrier((give, keep, moved, kv_spread))
+    kv_all = lax.all_to_all(kv_spread, TENSOR, 0, 0)
+    own_quarter = lax.all_gather(moved, "z", axis=0)
     arrived = lax.ppermute(give, "x_lo", SWAP)
-    kv_all = lax.all_to_all(jnp.broadcast_to(flat_kv[None], (8,) + flat_kv.shape), TENSOR, 0, 0)
-    own_quarter = lax.all_gather(moved, "z", axis=0)
-    arrived, own_quarter, kv_all = lax.optimization_barrier((arrived, own_quarter, kv_all))
+    arrived, own_quarter = lax.optimization_barrier((arrived, own_quarter))
     x_quarter = lax.ppermute(own_quarter, "x_lo", SWAP)
     core_quarter = lax.ppermute(own_quarter, "core", SWAP)
     quarters = add_pair(keep, arrived).astype(jnp.bfloat16)
     planes = lax.all_to_all(quarters, "z", 0, 0)
+    x_quarter, kv_all = lax.optimization_barrier((x_quarter, kv_all))
     far_quarter = lax.ppermute(x_quarter, "core", SWAP)
 
     near = jnp.where(x_at == 0, own_quarter, x_quarter), jnp.where(x_at == 0, x_quarter, own_quarter)
@@ -88,13 +94,13 @@
     )
     scaled = normed_grad * slice_gain
     inner = jnp.sum(scaled * slice_unit, axis=-1)
-    inner, planes = lax.optimization_barrier((inner, planes))
-    inner = lax.all_to_all(jnp.broadcast_to(inner[None], (8,) + inner.shape), TENSOR, 0, 0)
-    weight_grad = jnp.sum(planes.astype(jnp.float32), axis=0)
-    row_inner = jnp.sum(inner, axis=0)[:, :, None] / features
+    inner = jnp.sum(lax.all_gather(inner, "y", axis=0), axis=0)
+    inner = inner + lax.ppermute(inner, "x_hi", SWAP)
+    row_inner = inner[:, :, None] / features
     input_grads = row_scale * (scaled - slice_unit * row_inner)
     input_grads = jnp.where(live_mask[:, :, None], input_grads, 0.0).astype(jnp.bfloat16)
 
+    weight_grad = jnp.sum(planes.astype(jnp.float32), axis=0)
     mean_grad = weight_grad / 64**0.5
     new_moment_one = beta_one * moment_one + (1.0 - beta_one) * mean_grad
     new_moment_two = beta_two * moment_two + (1.0 - beta_two) * mean_grad * mean_grad

time: 123 us -> 113 us (0.919)
  waiting for transfers between devices: 22.1 us -> 6.47 us
  blocking collectives: 30.1 us -> 43.4 us
  starting transfers between devices: 50.3 us -> 46.2 us
    all_gather x0 -> x1, blocking collectives: none -> 11.9 us  [on_device(): inner = jnp.sum(lax.all_gather(inner, 'y', axis=0), axis=0)]
    all_to_all x3 -> x1, starting transfers between devices: 30.1 us -> 18.4 us  [on_device(): kv_all = lax.all_to_all(kv_spread, TENSOR, 0, 0)]
    all_to_all x3 -> x1, waiting for transfers between devices: 9.77 us -> 0.01 us  [on_device(): kv_all = lax.all_to_all(kv_spread, TENSOR, 0, 0)]
    ppermute x1, waiting for transfers between devices: 6.7 us -> 0.01 us  [on_device(): x_quarter = lax.ppermute(own_quarter, 'x_lo', SWAP)]
    ppermute x1 -> x3, starting transfers between devices: 0.65 us -> 7.26 us  [the longest x1 4.69 us: on_device(): inner = inner + lax.ppermute(inner, 'x_hi', SWAP)]
    ppermute x1 -> x3, waiting for transfers between devices: 0.01 us -> 4.9 us  [the longest x1 2.62 us: on_device(): arrived = lax.ppermute(give, 'core', SWAP)]
    all_to_all x1, waiting for transfers between devices: 3.71 us -> 0.01 us  [on_device(): planes = lax.all_to_all(quarters, 'z', 0, 0)]
    reshape x1 -> x0, local copies, waits for them, and re-layouts: 1.47 us -> none  [on_device(): partial = partial.astype(jnp.bfloat16).reshape(16, 2, 2, 64, columns)]
  transfers between devices with their start and end apart: 9 -> 9, of which waited for: 5 -> 3; matrix products, arithmetic and copies ran while one was open for 10% -> 12% of each run, Pallas kernels for 0% -> 0%
where the time goes in v3:
time: 113 us
  starting transfers between devices  46.2 us (41%)
  blocking collectives  43.4 us (38%)
  other arithmetic  9.57 us (8%)
  waiting for transfers between devices  6.47 us (6%)
  matrix products  3.74 us (3%)
  local copies, waits for them, and re-layouts  2.46 us (2%)
    all_gather x1, blocking collectives, on_device(): own_quarter = lax.all_gather(moved, 'z', axis=0)  31.4 us
    all_to_all x1, starting transfers between devices, on_device(): kv_all = lax.all_to_all(kv_spread, TENSOR, 0, 0)  18.4 us
    all_gather x1, blocking collectives, on_device(): inner = jnp.sum(lax.all_gather(inner, 'y', axis=0), axis=0)  11.9 us
    all_to_all x1, starting transfers between devices, on_device(): planes = lax.all_to_all(quarters, 'z', 0, 0)  10.3 us
    ppermute x1, starting transfers between devices, on_device(): inner = inner + lax.ppermute(inner, 'x_hi', SWAP)  4.69 us
    ppermute x1, starting transfers between devices, on_device(): arrived = lax.ppermute(give, 'x_lo', SWAP)  3.39 us
    ppermute x1, waiting for transfers between devices, on_device(): arrived = lax.ppermute(give, 'core', SWAP)  2.62 us
    reduce_sum x1, other arithmetic, on_device(): jnp.mean(wide_rows * wide_rows, axis=-1, keepdims=True) + norm_eps  2.58 us
  transfers between devices with their start and end apart: 9, of which 3 were waited for; matrix products, arithmetic and copies ran while one was open for 12% of the time, Pallas kernels for 0%

profile of v3, /device:TPU:32, one launch (start us, length us, event | category | flops | bytes accessed | tf_op | source)
XLA Modules:
  0.0 112.6 jit_solution(6494932114256871123)
XLA Ops:
  0.6 0.8 convert
  1.5 0.7 collective-permute-start
  2.2 2.3 %broadcast_in_dim.38 = bf16[8,384,256]{2,1,0:T(8,128)(2,1)} broadcast(bf16[384,256]{1,0:T(8,128)(2,1)} %bitcast.77), dimensions={1,2} | broadcast | bytes 1769472 | tf_op jit(solution)/shard_map/broadcast_in_dim | solution.py:44
  4.5 2.6 %fusion = f32[3,128]{1,0:T(4,128)S(1)} fusion(bf16[3,128,4096]{2,1,0:T(8,128)(2,1)} %param.8), kind=kLoop, calls=%fused_computation.2 | loop fusion | flops 4718208 | bytes 3147264 | tf_op jit(solution)/shard_map/reduce_sum | solution.py:51
  7.1 0.1 fusion.15
  7.2 1.6 %fusion.3 = bf16[4096,256]{1,0:T(8,128)(2,1)S(1)} fusion(bf16[3,128,4096]{2,1,0:T(8,128)(2,1)S(1)} %copy-done, f32[4096]{0:T(1024)S(1)} %copy-done.7, f32[3,128]{1,0:T(4,128)S(1)} %add_rsqrt_fusion, bf16[3,128,256]{2,1,0:T(8,128)(2,1)S(1)} %copy-done.2, pred[3,128]{1,0:T(4,128)(4,1)S(1)} %fusion.15), kind=kOutput, calls=%fused_computation.6 | convolution fusion | flops 812744704 | bytes 5457792 | tf_op jit(solution)/shard_map/dot_general | solution.py:53
  8.9 0.1 fusion.8
  9.0 0.1 fusion.9
  9.1 1.9 %collective-permute-start.1 = (bf16[2,16,64,256]{3,2,0,1:T(8,128)(2,1)S(1)}, bf16[2,16,64,256]{3,2,0,1:T(8,128)(2,1)S(1)}, u32[]{:S(2)}, u32[]{:S(2)}) collective-permute-start(bf16[2,16,64,256]{3,2,0,1:T(8,128)(2,1)S(1)} %fusion.9), channel_id=1, source_target_pairs={{0,1},{1,0},{2,3},{3,2},{4,5},{5,4},{6,7},{7,6},{8,9},{9,8},{10,11... | collective-permute-start | bytes 3145736 | tf_op jit(solution)/shard_map/ppermute | solution.py:64
  11.1 2.6 %collective-permute-done.1 = bf16[2,16,64,256]{3,2,0,1:T(8,128)(2,1)S(1)} collective-permute-done((bf16[2,16,64,256]{3,2,0,1:T(8,128)(2,1)S(1)}, bf16[2,16,64,256]{3,2,0,1:T(8,128)(2,1)S(1)}, u32[]{:S(2)}, u32[]{:S(2)}) %collective-permute-start.1) | collective-permute-done | bytes 1048608 | tf_op jit(solution)/shard_map/ppermute | solution.py:64
  13.7 0.4 add_convert_fusion
  14.1 0.1 fusion.10
  14.1 0.1 fusion.11
  14.2 18.4 %all-to-all-start = ((bf16[8,384,256]{2,1,0:T(8,128)(2,1)}), bf16[8,384,256]{2,1,0:T(8,128)(2,1)S(1)}, u32[]{:S(2)}, u32[]{:S(2)}) async-start(bf16[8,384,256]{2,1,0:T(8,128)(2,1)} %broadcast_in_dim.38), calls=%async_computation | async-start | bytes 3145728 | tf_op jit(solution)/shard_map/all_to_all | solution.py:69
  32.6 3.4 %collective-permute-start.2 = (bf16[16,64,256]{2,1,0:T(8,128)(2,1)S(1)}, bf16[16,64,256]{2,1,0:T(8,128)(2,1)S(1)}, u32[]{:S(2)}, u32[]{:S(2)}) collective-permute-start(bf16[16,64,256]{2,1,0:T(8,128)(2,1)S(1)} %fusion.11), channel_id=1, source_target_pairs={{0,2},{2,0},{1,3},{3,1},{4,6},{6,4},{5,7},{7,5},{8,10},{10,8},{9,1... | collective-permute-start | bytes 1572872 | tf_op jit(solution)/shard_map/ppermute | solution.py:71
  36.0 31.4 %all-gather = bf16[1024,256]{1,0:T(8,128)(2,1)S(1)} all-gather(bf16[64,256]{1,0:T(8,128)(2,1)S(1)} %collective-permute-done), channel_id=2, replica_groups=mesh['x_hi'=2,'y'=4,'z'=16,'x_lo'=2,'core'=2] {'z'}, dimensions={0}, use_global_device_ids=true | all-gather | bytes 557056 | tf_op jit(solution)/shard_map/all_gather | solution.py:70
  67.4 2.4 %collective-permute-start.3 = (bf16[16,64,256]{2,1,0:T(8,128)(2,1)S(1)}, bf16[16,64,256]{2,1,0:T(8,128)(2,1)S(1)}, u32[]{:S(2)}, u32[]{:S(2)}) collective-permute-start(bf16[16,64,256]{2,1,0:T(8,128)(2,1)S(1)} %bitcast.68), channel_id=1, source_target_pairs={{0,2},{2,0},{1,3},{3,1},{4,6},{6,4},{5,7},{7,5},{8,10},{10,8},{9,1... | collective-permute-start | bytes 1572872 | tf_op jit(solution)/shard_map/ppermute | solution.py:73
  69.9 1.0 add_convert_fusion.1
  70.8 10.3 %all-to-all-start.1 = ((bf16[16,64,256]{2,1,0:T(8,128)(2,1)}), bf16[16,64,256]{2,1,0:T(8,128)(2,1)S(1)}, u32[]{:S(2)}, u32[]{:S(2)}) async-start(bf16[16,64,256]{2,1,0:T(8,128)(2,1)} %add_convert_fusion.1), calls=%async_computation.1 | async-start | bytes 1048576 | tf_op jit(solution)/shard_map/all_to_all | solution.py:76
  81.2 1.9 %collective-permute-start.4 = (bf16[16,64,256]{2,1,0:T(8,128)(2,1)S(1)}, bf16[16,64,256]{2,1,0:T(8,128)(2,1)}, u32[]{:S(2)}, u32[]{:S(2)}) collective-permute-start(bf16[16,64,256]{2,1,0:T(8,128)(2,1)S(1)} %bitcast.69), channel_id=1, source_target_pairs={{0,1},{1,0},{2,3},{3,2},{4,5},{5,4},{6,7},{7,6},{8,9},{9,8},{10,11... | collective-permute-start | bytes 1572872 | tf_op jit(solution)/shard_map/ppermute | solution.py:74
  83.1 2.4 %collective-permute-start.5 = (bf16[16,64,256]{2,1,0:T(8,128)(2,1)S(1)}, bf16[16,64,256]{2,1,0:T(8,128)(2,1)}, u32[]{:S(2)}, u32[]{:S(2)}) collective-permute-start(bf16[16,64,256]{2,1,0:T(8,128)(2,1)S(1)} %collective-permute-done.3), channel_id=1, source_target_pairs={{0,1},{1,0},{2,3},{3,2},{4,5},{5,4},{6,7},{7,6},{8,9},{9,8},{10,11... | collective-permute-start | bytes 1572872 | tf_op jit(solution)/shard_map/ppermute | solution.py:78
  85.5 0.1 dynamic_slice.6
  85.6 1.6 %collective-permute-done.5 = bf16[16,64,256]{2,1,0:T(8,128)(2,1)} collective-permute-done((bf16[16,64,256]{2,1,0:T(8,128)(2,1)S(1)}, bf16[16,64,256]{2,1,0:T(8,128)(2,1)}, u32[]{:S(2)}, u32[]{:S(2)}) %collective-permute-start.5) | collective-permute-done | bytes 524320 | tf_op jit(solution)/shard_map/ppermute | solution.py:78
  87.1 1.4 %broadcast_select_fusion.7 = (bf16[16,64,256]{2,1,0:T(8,128)(2,1)S(1)}, bf16[16,64,256]{2,1,0:T(8,128)(2,1)S(1)}, bf16[16,64,256]{2,1,0:T(8,128)(2,1)S(1)}, bf16[16,64,256]{2,1,0:T(8,128)(2,1)S(1)}) fusion(pred[]{:T(512)S(6)} %eq.7, bf16[16,64,256]{2,1,0:T(8,128)(2,1)S(1)} %bitcast.70, bf16[16,64,256]{2,1,0:T(8,128)(2,1)S(1)} %collective-permute-done.3, ...), kind=kLoop, calls=%fused_computation.33 | loop fusion | flops 2097152 | bytes 4194307 | tf_op jit(solution)/shard_map/jit(_where)/select_n | solution.py:83
  88.5 0.3 pad_maximum_fusion
  88.8 2.1 %multiply_reduce_fusion = (f32[3,128]{1,0:T(4,128)S(1)}, f32[3,128,512]{2,1,0:T(8,128)S(1)}) fusion(f32[3,128]{1,0:T(4,128)S(1)} %add_rsqrt_fusion, bf16[3,128,4096]{2,1,0:T(8,128)(2,1)} %param.8, s32[]{:T(128)S(6)} %select_n.108, f32[512]{0:T(512)S(1)} %dynamic_slice.6, bf16[3,128,8,256]{3,1,0,2:T(8,128)(2,1)S(1)} %bitcast.76, ...), kind=kOutput, calls=%fused_computation.21 | convolution fusion | flops 806289024 | bytes 4854788 | tf_op jit(solution)/shard_map/dot_general | solution.py:87
  90.9 11.9 %all-gather.2 = f32[4,3,128]{2,1,0:T(4,128)S(1)} all-gather(f32[1,3,128]{2,1,0:T(4,128)S(1)} %bitcast.78), channel_id=3, replica_groups=mesh['x_hi'=2,'y'=4,'z'=16,'x_lo'=2,'core'=2] {'y'}, dimensions={0}, use_global_device_ids=true | all-gather | bytes 7680 | tf_op jit(solution)/shard_map/all_gather | solution.py:97
  102.9 4.7 %collective-permute-start.6 = (f32[3,128]{1,0:T(4,128)S(1)}, f32[3,128]{1,0:T(4,128)S(1)}, u32[]{:S(2)}, u32[]{:S(2)}) collective-permute-start(f32[3,128]{1,0:T(4,128)S(1)} %reduce_sum.38), channel_id=1, source_target_pairs={{0,256},{256,0},{1,257},{257,1},{2,258},{258,2},{3,259},{259,3},{4... | collective-permute-start | bytes 4616 | tf_op jit(solution)/shard_map/ppermute | solution.py:98
  107.6 2.3 %collective-permute-done.6 = f32[3,128]{1,0:T(4,128)S(1)} collective-permute-done((f32[3,128]{1,0:T(4,128)S(1)}, f32[3,128]{1,0:T(4,128)S(1)}, u32[]{:S(2)}, u32[]{:S(2)}) %collective-permute-start.6) | collective-permute-done | bytes 1568 | tf_op jit(solution)/shard_map/ppermute | solution.py:98
  109.9 2.0 %select_convert_fusion = bf16[3,128,512]{2,1,0:T(8,128)(2,1)} fusion(f32[3,128,512]{2,1,0:T(8,128)S(1)} %get-tuple-element.38, f32[3,128]{1,0:T(4,128)S(1)} %add_multiply_fusion, f32[3,128]{1,0:T(4,128)S(1)} %add_rsqrt_fusion, pred[3,128]{1,0:T(4,128)(4,1)S(1)} %fusion.15, bf16[3,128,4096]{2,1,0:T(8,128)(2,1)} %param.8, s32[]{:T(128)S(6)} %select_n.108), kind=kLoop, calls=%fused_computation.20 | loop fusion | flops 1376256 | bytes 1576324 | tf_op jit(solution)/shard_map/convert_element_type | solution.py:101
  111.8 0.1 convert_reduce_fusion
  111.9 0.7 divide_subtract_fusion
  (25 shorter events, 0.1 us)
Async XLA Ops:
  1.5 7.6 %collective-permute-start = (bf16[64,256]{1,0:T(8,128)(2,1)S(1)}, bf16[64,256]{1,0:T(8,128)(2,1)S(1)}, u32[]{:S(2)}, u32[]{:S(2)}) collective-permute-start(bf16[64,256]{1,0:T(8,128)(2,1)S(1)} %convert), channel_id=1, source_target_pairs={{0,0},{1,1},{2,2},{3,3},{4,4},{5,5},{6,6},{7,7},{8,64},{9,65},{10,... | collective-permute-start | bytes 98312 | tf_op jit(solution)/shard_map/ppermute | solution.py:42
  2.1 5.0 %copy-start.5 = (s32[3,128]{1,0:T(4,128)S(1)}, s32[3,128]{1,0:T(4,128)}, u32[]{:S(2)}) copy-start(s32[3,128]{1,0:T(4,128)} %param.15) | copy-start | bytes 4612
  2.2 5.0 %copy-start.6 = (s32[3,1]{0,1:T(1,128)S(1)}, s32[3,1]{0,1:T(1,128)}, u32[]{:S(2)}) copy-start(s32[3,1]{0,1:T(1,128)} %param.14) | copy-start | bytes 40
  2.2 5.1 %copy-start = (bf16[3,128,4096]{2,1,0:T(8,128)(2,1)S(1)}, bf16[3,128,4096]{2,1,0:T(8,128)(2,1)}, u32[]{:S(2)}) copy-start(bf16[3,128,4096]{2,1,0:T(8,128)(2,1)} %param.8) | copy-start | bytes 9437188
  2.2 5.0 %copy-start.2 = (bf16[3,128,256]{2,1,0:T(8,128)(2,1)S(1)}, bf16[3,128,256]{2,1,0:T(8,128)(2,1)}, u32[]{:S(2)}) copy-start(bf16[3,128,256]{2,1,0:T(8,128)(2,1)} %param.9) | copy-start | bytes 589828
  2.2 5.0 %copy-start.7 = (f32[4096]{0:T(1024)S(1)}, f32[4096]{0:T(1024)}, u32[]{:S(2)}) copy-start(f32[4096]{0:T(1024)} %param.10) | copy-start | bytes 49156
  9.1 4.6 %collective-permute-start.1 = (bf16[2,16,64,256]{3,2,0,1:T(8,128)(2,1)S(1)}, bf16[2,16,64,256]{3,2,0,1:T(8,128)(2,1)S(1)}, u32[]{:S(2)}, u32[]{:S(2)}) collective-permute-start(bf16[2,16,64,256]{3,2,0,1:T(8,128)(2,1)S(1)} %fusion.9), channel_id=1, source_target_pairs={{0,1},{1,0},{2,3},{3,2},{4,5},{5,4},{6,7},{7,6},{8,9},{9,8},{10,11... | collective-permute-start | bytes 3145736 | tf_op jit(solution)/shard_map/ppermute | solution.py:64
  14.2 56.6 %all-to-all-start = ((bf16[8,384,256]{2,1,0:T(8,128)(2,1)}), bf16[8,384,256]{2,1,0:T(8,128)(2,1)S(1)}, u32[]{:S(2)}, u32[]{:S(2)}) async-start(bf16[8,384,256]{2,1,0:T(8,128)(2,1)} %broadcast_in_dim.38), calls=%async_computation | async-start | bytes 3145728 | tf_op jit(solution)/shard_map/all_to_all | solution.py:69
  32.6 34.8 %collective-permute-start.2 = (bf16[16,64,256]{2,1,0:T(8,128)(2,1)S(1)}, bf16[16,64,256]{2,1,0:T(8,128)(2,1)S(1)}, u32[]{:S(2)}, u32[]{:S(2)}) collective-permute-start(bf16[16,64,256]{2,1,0:T(8,128)(2,1)S(1)} %fusion.11), channel_id=1, source_target_pairs={{0,2},{2,0},{1,3},{3,1},{4,6},{6,4},{5,7},{7,5},{8,10},{10,8},{9,1... | collective-permute-start | bytes 1572872 | tf_op jit(solution)/shard_map/ppermute | solution.py:71
  67.4 15.6 %collective-permute-start.3 = (bf16[16,64,256]{2,1,0:T(8,128)(2,1)S(1)}, bf16[16,64,256]{2,1,0:T(8,128)(2,1)S(1)}, u32[]{:S(2)}, u32[]{:S(2)}) collective-permute-start(bf16[16,64,256]{2,1,0:T(8,128)(2,1)S(1)} %bitcast.68), channel_id=1, source_target_pairs={{0,2},{2,0},{1,3},{3,1},{4,6},{6,4},{5,7},{7,5},{8,10},{10,8},{9,1... | collective-permute-start | bytes 1572872 | tf_op jit(solution)/shard_map/ppermute | solution.py:73
  70.8 41.0 %all-to-all-start.1 = ((bf16[16,64,256]{2,1,0:T(8,128)(2,1)}), bf16[16,64,256]{2,1,0:T(8,128)(2,1)S(1)}, u32[]{:S(2)}, u32[]{:S(2)}) async-start(bf16[16,64,256]{2,1,0:T(8,128)(2,1)} %add_convert_fusion.1), calls=%async_computation.1 | async-start | bytes 1048576 | tf_op jit(solution)/shard_map/all_to_all | solution.py:76
  81.2 4.4 %collective-permute-start.4 = (bf16[16,64,256]{2,1,0:T(8,128)(2,1)S(1)}, bf16[16,64,256]{2,1,0:T(8,128)(2,1)}, u32[]{:S(2)}, u32[]{:S(2)}) collective-permute-start(bf16[16,64,256]{2,1,0:T(8,128)(2,1)S(1)} %bitcast.69), channel_id=1, source_target_pairs={{0,1},{1,0},{2,3},{3,2},{4,5},{5,4},{6,7},{7,6},{8,9},{9,8},{10,11... | collective-permute-start | bytes 1572872 | tf_op jit(solution)/shard_map/ppermute | solution.py:74
  83.1 4.1 %collective-permute-start.5 = (bf16[16,64,256]{2,1,0:T(8,128)(2,1)S(1)}, bf16[16,64,256]{2,1,0:T(8,128)(2,1)}, u32[]{:S(2)}, u32[]{:S(2)}) collective-permute-start(bf16[16,64,256]{2,1,0:T(8,128)(2,1)S(1)} %collective-permute-done.3), channel_id=1, source_target_pairs={{0,1},{1,0},{2,3},{3,2},{4,5},{5,4},{6,7},{7,6},{8,9},{9,8},{10,11... | collective-permute-start | bytes 1572872 | tf_op jit(solution)/shard_map/ppermute | solution.py:78
  90.9 21.0 %copy-start.1 = (f32[64,256]{1,0:T(8,128)S(1)}, f32[64,256]{1,0:T(8,128)}, u32[]{:S(2)}) copy-start(f32[64,256]{1,0:T(8,128)} %param.11) | copy-start | bytes 196612
  90.9 21.0 %copy-start.3 = (f32[64,256]{1,0:T(8,128)S(1)}, f32[64,256]{1,0:T(8,128)}, u32[]{:S(2)}) copy-start(f32[64,256]{1,0:T(8,128)} %param.12) | copy-start | bytes 196612
  90.9 21.0 %copy-start.4 = (f32[64,256]{1,0:T(8,128)S(1)}, f32[64,256]{1,0:T(8,128)}, u32[]{:S(2)}) copy-start(f32[64,256]{1,0:T(8,128)} %param.13) | copy-start | bytes 196612
  102.9 7.0 %collective-permute-start.6 = (f32[3,128]{1,0:T(4,128)S(1)}, f32[3,128]{1,0:T(4,128)S(1)}, u32[]{:S(2)}, u32[]{:S(2)}) collective-permute-start(f32[3,128]{1,0:T(4,128)S(1)} %reduce_sum.38), channel_id=1, source_target_pairs={{0,256},{256,0},{1,257},{257,1},{2,258},{258,2},{3,259},{259,3},{4... | collective-permute-start | bytes 4616 | tf_op jit(solution)/shard_map/ppermute | solution.py:98

commit v4 on v3

--- a/solution.py
+++ b/solution.py
@@ -62,6 +62,10 @@
     keep = jnp.where(core_at == 0, partial[0], partial[1])
     give, keep, moved = lax.optimization_barrier((give, keep, moved))
     arrived = lax.ppermute(give, "core", SWAP)
+    slice_unit = (
+        lax.dynamic_slice_in_dim(activations, member * 512, 512, 2).astype(jnp.float32) * row_scale
+    )
+    arrived, slice_unit = lax.optimization_barrier((arrived, slice_unit))
     halves = add_pair(keep, arrived).astype(jnp.bfloat16)
     keep = jnp.where(x_at == 0, halves[0], halves[1])
     give = jnp.where(x_at == 0, halves[1], halves[0])
@@ -89,17 +93,10 @@
     ).reshape(batches, tok_rows, 512)
     offset = member * 512
     slice_gain = lax.dynamic_slice_in_dim(norm_gain, offset, 512, 0)
-    slice_unit = (
-        lax.dynamic_slice_in_dim(activations, offset, 512, 2).astype(jnp.float32) * row_scale
-    )
     scaled = normed_grad * slice_gain
     inner = jnp.sum(scaled * slice_unit, axis=-1)
     inner = jnp.sum(lax.all_gather(inner, "y", axis=0), axis=0)
     inner = inner + lax.ppermute(inner, "x_hi", SWAP)
-    row_inner = inner[:, :, None] / features
-    input_grads = row_scale * (scaled - slice_unit * row_inner)
-    input_grads = jnp.where(live_mask[:, :, None], input_grads, 0.0).astype(jnp.bfloat16)
-
     weight_grad = jnp.sum(planes.astype(jnp.float32), axis=0)
     mean_grad = weight_grad / 64**0.5
     new_moment_one = beta_one * moment_one + (1.0 - beta_one) * mean_grad
@@ -107,6 +104,15 @@
     first_fixed = new_moment_one / (1.0 - beta_one**adam_step)
     second_fixed = new_moment_two / (1.0 - beta_two**adam_step)
     new_master = master - learn_rate * first_fixed / (jnp.sqrt(second_fixed) + adam_eps)
+    inner, new_master, new_moment_one, new_moment_two = lax.optimization_barrier(
+        (inner, new_master, new_moment_one, new_moment_two)
+    )
+    plain = jnp.where(live_mask[:, :, None], row_scale * scaled, 0.0)
+    along = jnp.where(live_mask[:, :, None], row_scale * slice_unit, 0.0)
+    inner, plain, along = lax.optimization_barrier((inner, plain, along))
+    row_inner = inner[:, :, None] / features
+    input_grads = (plain - along * row_inner).astype(jnp.bfloat16)
+
     return (input_grads, new_master, new_moment_one, new_moment_two)
 
 

time: 113 us -> 111 us (0.982)
  the two profiles are of different devices: /device:TPU:32 before, /device:TPU:4 now
where the time goes in v4:
time: 111 us
  starting transfers between devices  43.3 us (39%)
  blocking collectives  42.7 us (38%)
  other arithmetic  9.7 us (9%)
  waiting for transfers between devices  7.74 us (7%)
  matrix products  4.05 us (4%)
  local copies, waits for them, and re-layouts  2.46 us (2%)
    all_gather x1, blocking collectives, on_device(): own_quarter = lax.all_gather(moved, 'z', axis=0)  31.7 us
    ppermute x1, starting transfers between devices, on_device(): lax.ppermute(master, TENSOR + DP, slice_owner_pairs()).astype(jnp.bfloat16)  15.7 us
    all_gather x1, blocking collectives, on_device(): inner = jnp.sum(lax.all_gather(inner, 'y', axis=0), axis=0)  11 us
    all_to_all x1, starting transfers between devices, on_device(): planes = lax.all_to_all(quarters, 'z', 0, 0)  8.27 us
    all_to_all x1, starting transfers between devices, on_device(): kv_all = lax.all_to_all(kv_spread, TENSOR, 0, 0)  4.83 us
    ppermute x1, waiting for transfers between devices, on_device(): inner = inner + lax.ppermute(inner, 'x_hi', SWAP)  4.59 us
    ppermute x1, starting transfers between devices, on_device(): arrived = lax.ppermute(give, 'x_lo', SWAP)  3.99 us
    reduce_sum x1, other arithmetic, on_device(): jnp.mean(wide_rows * wide_rows, axis=-1, keepdims=True) + norm_eps  2.58 us
  transfers between devices with their start and end apart: 9, of which 3 were waited for; matrix products, arithmetic and copies ran while one was open for 12% of the time, Pallas kernels for 0%

profile of v4, /device:TPU:4, one launch (start us, length us, event | category | flops | bytes accessed | tf_op | source)
XLA Modules:
  0.0 110.9 jit_solution(8678188867610956875)
XLA Ops:
  0.6 0.8 convert
  1.5 15.7 %collective-permute-start = (bf16[64,256]{1,0:T(8,128)(2,1)S(1)}, bf16[64,256]{1,0:T(8,128)(2,1)S(1)}, u32[]{:S(2)}, u32[]{:S(2)}) collective-permute-start(bf16[64,256]{1,0:T(8,128)(2,1)S(1)} %convert), channel_id=1, source_target_pairs={{0,0},{1,1},{2,2},{3,3},{4,4},{5,5},{6,6},{7,7},{8,64},{9,65},{10,... | collective-permute-start | bytes 98312 | tf_op jit(solution)/shard_map/ppermute | solution.py:42
  17.2 2.3 %broadcast_in_dim.42 = bf16[8,384,256]{2,1,0:T(8,128)(2,1)} broadcast(bf16[384,256]{1,0:T(8,128)(2,1)} %bitcast.76), dimensions={1,2} | broadcast | bytes 1769472 | tf_op jit(solution)/shard_map/broadcast_in_dim | solution.py:44
  19.5 2.6 %fusion = f32[3,128]{1,0:T(4,128)S(1)} fusion(bf16[3,128,4096]{2,1,0:T(8,128)(2,1)} %param.8), kind=kLoop, calls=%fused_computation.2 | loop fusion | flops 4718208 | bytes 3147264 | tf_op jit(solution)/shard_map/reduce_sum | solution.py:51
  22.1 0.1 fusion.15
  22.2 1.6 %fusion.3 = bf16[4096,256]{1,0:T(8,128)(2,1)S(1)} fusion(bf16[3,128,4096]{2,1,0:T(8,128)(2,1)S(1)} %copy-done, f32[4096]{0:T(1024)S(1)} %copy-done.7, f32[3,128]{1,0:T(4,128)S(1)} %add_rsqrt_fusion, bf16[3,128,256]{2,1,0:T(8,128)(2,1)S(1)} %copy-done.2, pred[3,128]{1,0:T(4,128)(4,1)S(1)} %fusion.15), kind=kOutput, calls=%fused_computation.6 | convolution fusion | flops 812744704 | bytes 5457792 | tf_op jit(solution)/shard_map/dot_general | solution.py:53
  23.9 0.1 fusion.8
  24.0 1.1 fusion.9
  25.1 1.9 %collective-permute-start.1 = (bf16[2,16,64,256]{3,2,0,1:T(8,128)(2,1)}, bf16[2,16,64,256]{3,2,0,1:T(8,128)(2,1)S(1)}, u32[]{:S(2)}, u32[]{:S(2)}) collective-permute-start(bf16[2,16,64,256]{3,2,0,1:T(8,128)(2,1)} %fusion.9), channel_id=1, source_target_pairs={{0,1},{1,0},{2,3},{3,2},{4,5},{5,4},{6,7},{7,6},{8,9},{9,8},{10,11... | collective-permute-start | bytes 3145736 | tf_op jit(solution)/shard_map/ppermute | solution.py:64
  27.0 1.1 %convert_multiply_fusion.2 = f32[3,128,512]{2,1,0:T(8,128)S(1)} fusion(f32[3,128]{1,0:T(4,128)S(1)} %add_rsqrt_fusion, bf16[3,128,4096]{2,1,0:T(8,128)(2,1)} %param.8, s32[]{:T(128)S(6)} %select_n.96), kind=kLoop, calls=%fused_computation.24 | loop fusion | flops 393216 | bytes 1181188 | tf_op jit(solution)/shard_map/mul | solution.py:66
  28.1 1.7 %collective-permute-done.1 = bf16[2,16,64,256]{3,2,0,1:T(8,128)(2,1)S(1)} collective-permute-done((bf16[2,16,64,256]{3,2,0,1:T(8,128)(2,1)}, bf16[2,16,64,256]{3,2,0,1:T(8,128)(2,1)S(1)}, u32[]{:S(2)}, u32[]{:S(2)}) %collective-permute-start.1) | collective-permute-done | bytes 1048608 | tf_op jit(solution)/shard_map/ppermute | solution.py:64
  29.8 0.4 add_convert_fusion
  30.3 4.8 %all-to-all-start = ((bf16[8,384,256]{2,1,0:T(8,128)(2,1)}), bf16[8,384,256]{2,1,0:T(8,128)(2,1)}, u32[]{:S(2)}, u32[]{:S(2)}) async-start(bf16[8,384,256]{2,1,0:T(8,128)(2,1)} %broadcast_in_dim.42), calls=%async_computation | async-start | bytes 3145728 | tf_op jit(solution)/shard_map/all_to_all | solution.py:73
  35.2 4.0 %collective-permute-start.2 = (bf16[16,64,256]{2,1,0:T(8,128)(2,1)S(1)}, bf16[16,64,256]{2,1,0:T(8,128)(2,1)S(1)}, u32[]{:S(2)}, u32[]{:S(2)}) collective-permute-start(bf16[16,64,256]{2,1,0:T(8,128)(2,1)S(1)} %fusion.11), channel_id=1, source_target_pairs={{0,2},{2,0},{1,3},{3,1},{4,6},{6,4},{5,7},{7,5},{8,10},{10,8},{9,1... | collective-permute-start | bytes 1572872 | tf_op jit(solution)/shard_map/ppermute | solution.py:75
  39.2 31.7 %all-gather = bf16[1024,256]{1,0:T(8,128)(2,1)S(1)} all-gather(bf16[64,256]{1,0:T(8,128)(2,1)S(1)} %collective-permute-done), channel_id=2, replica_groups=mesh['x_hi'=2,'y'=4,'z'=16,'x_lo'=2,'core'=2] {'z'}, dimensions={0}, use_global_device_ids=true | all-gather | bytes 557056 | tf_op jit(solution)/shard_map/all_gather | solution.py:74
  70.9 1.9 %collective-permute-start.3 = (bf16[16,64,256]{2,1,0:T(8,128)(2,1)S(1)}, bf16[16,64,256]{2,1,0:T(8,128)(2,1)S(1)}, u32[]{:S(2)}, u32[]{:S(2)}) collective-permute-start(bf16[16,64,256]{2,1,0:T(8,128)(2,1)S(1)} %bitcast.68), channel_id=1, source_target_pairs={{0,2},{2,0},{1,3},{3,1},{4,6},{6,4},{5,7},{7,5},{8,10},{10,8},{9,1... | collective-permute-start | bytes 1572872 | tf_op jit(solution)/shard_map/ppermute | solution.py:77
  72.8 1.0 add_convert_fusion.1
  73.8 8.3 %all-to-all-start.1 = ((bf16[16,64,256]{2,1,0:T(8,128)(2,1)}), bf16[16,64,256]{2,1,0:T(8,128)(2,1)S(1)}, u32[]{:S(2)}, u32[]{:S(2)}) async-start(bf16[16,64,256]{2,1,0:T(8,128)(2,1)} %add_convert_fusion.1), calls=%async_computation.1 | async-start | bytes 1048576 | tf_op jit(solution)/shard_map/all_to_all | solution.py:80
  82.1 1.9 %collective-permute-start.4 = (bf16[16,64,256]{2,1,0:T(8,128)(2,1)S(1)}, bf16[16,64,256]{2,1,0:T(8,128)(2,1)S(1)}, u32[]{:S(2)}, u32[]{:S(2)}) collective-permute-start(bf16[16,64,256]{2,1,0:T(8,128)(2,1)S(1)} %bitcast.69), channel_id=1, source_target_pairs={{0,1},{1,0},{2,3},{3,2},{4,5},{5,4},{6,7},{7,6},{8,9},{9,8},{10,11... | collective-permute-start | bytes 1572872 | tf_op jit(solution)/shard_map/ppermute | solution.py:78
  84.0 2.4 %collective-permute-start.5 = (bf16[16,64,256]{2,1,0:T(8,128)(2,1)S(1)}, bf16[16,64,256]{2,1,0:T(8,128)(2,1)S(1)}, u32[]{:S(2)}, u32[]{:S(2)}) collective-permute-start(bf16[16,64,256]{2,1,0:T(8,128)(2,1)S(1)} %collective-permute-done.3), channel_id=1, source_target_pairs={{0,1},{1,0},{2,3},{3,2},{4,5},{5,4},{6,7},{7,6},{8,9},{9,8},{10,11... | collective-permute-start | bytes 1572872 | tf_op jit(solution)/shard_map/ppermute | solution.py:82
  86.4 0.1 dynamic_slice.7
  86.5 1.4 %collective-permute-done.5 = bf16[16,64,256]{2,1,0:T(8,128)(2,1)S(1)} collective-permute-done((bf16[16,64,256]{2,1,0:T(8,128)(2,1)S(1)}, bf16[16,64,256]{2,1,0:T(8,128)(2,1)S(1)}, u32[]{:S(2)}, u32[]{:S(2)}) %collective-permute-start.5) | collective-permute-done | bytes 524320 | tf_op jit(solution)/shard_map/ppermute | solution.py:82
  87.9 0.2 broadcast_select_fusion.7
  88.1 0.3 pad_maximum_fusion
  88.4 2.4 %fusion.7 = f32[3,128,512]{2,1,0:T(8,128)S(1)} fusion(bf16[3,128,8,256]{3,1,0,2:T(8,128)(2,1)} %bitcast.19, bf16[8,512,256,1]{2,1,3,0:T(8,128)(2,1)S(1)} %bitcast.71, f32[512]{0:T(512)S(1)} %dynamic_slice.7), kind=kOutput, calls=%fused_computation.13 | convolution fusion | flops 805502976 | bytes 4458496 | tf_op jit(solution)/shard_map/dot_general | solution.py:91
  90.8 0.3 multiply_select_fusion
  91.2 11.0 %all-gather.2 = f32[4,3,128]{2,1,0:T(4,128)S(1)} all-gather(f32[1,3,128]{2,1,0:T(4,128)S(1)} %bitcast.77), channel_id=3, replica_groups=mesh['x_hi'=2,'y'=4,'z'=16,'x_lo'=2,'core'=2] {'y'}, dimensions={0}, use_global_device_ids=true | all-gather | bytes 7680 | tf_op jit(solution)/shard_map/all_gather | solution.py:98
  102.2 2.4 %collective-permute-start.6 = (f32[3,128]{1,0:T(4,128)S(1)}, f32[3,128]{1,0:T(4,128)S(1)}, u32[]{:S(2)}, u32[]{:S(2)}) collective-permute-start(f32[3,128]{1,0:T(4,128)S(1)} %reduce_sum.38), channel_id=1, source_target_pairs={{0,256},{256,0},{1,257},{257,1},{2,258},{258,2},{3,259},{259,3},{4... | collective-permute-start | bytes 4616 | tf_op jit(solution)/shard_map/ppermute | solution.py:99
  104.6 4.6 %collective-permute-done.6 = f32[3,128]{1,0:T(4,128)S(1)} collective-permute-done((f32[3,128]{1,0:T(4,128)S(1)}, f32[3,128]{1,0:T(4,128)S(1)}, u32[]{:S(2)}, u32[]{:S(2)}) %collective-permute-start.6) | collective-permute-done | bytes 1568 | tf_op jit(solution)/shard_map/ppermute | solution.py:99
  109.2 0.1 convert_reduce_fusion
  109.3 0.7 divide_subtract_fusion
  110.0 0.9 subtract_convert_fusion
  (28 shorter events, 0.2 us)
Async XLA Ops:
  1.5 23.6 %collective-permute-start = (bf16[64,256]{1,0:T(8,128)(2,1)S(1)}, bf16[64,256]{1,0:T(8,128)(2,1)S(1)}, u32[]{:S(2)}, u32[]{:S(2)}) collective-permute-start(bf16[64,256]{1,0:T(8,128)(2,1)S(1)} %convert), channel_id=1, source_target_pairs={{0,0},{1,1},{2,2},{3,3},{4,4},{5,5},{6,6},{7,7},{8,64},{9,65},{10,... | collective-permute-start | bytes 98312 | tf_op jit(solution)/shard_map/ppermute | solution.py:42
  17.1 5.0 %copy-start.5 = (s32[3,128]{1,0:T(4,128)S(1)}, s32[3,128]{1,0:T(4,128)}, u32[]{:S(2)}) copy-start(s32[3,128]{1,0:T(4,128)} %param.15) | copy-start | bytes 4612
  17.2 5.0 %copy-start.6 = (s32[3,1]{0,1:T(1,128)S(1)}, s32[3,1]{0,1:T(1,128)}, u32[]{:S(2)}) copy-start(s32[3,1]{0,1:T(1,128)} %param.14) | copy-start | bytes 40
  17.2 5.1 %copy-start = (bf16[3,128,4096]{2,1,0:T(8,128)(2,1)S(1)}, bf16[3,128,4096]{2,1,0:T(8,128)(2,1)}, u32[]{:S(2)}) copy-start(bf16[3,128,4096]{2,1,0:T(8,128)(2,1)} %param.8) | copy-start | bytes 9437188
  17.2 5.0 %copy-start.2 = (bf16[3,128,256]{2,1,0:T(8,128)(2,1)S(1)}, bf16[3,128,256]{2,1,0:T(8,128)(2,1)}, u32[]{:S(2)}) copy-start(bf16[3,128,256]{2,1,0:T(8,128)(2,1)} %param.9) | copy-start | bytes 589828
  17.2 5.0 %copy-start.7 = (f32[4096]{0:T(1024)S(1)}, f32[4096]{0:T(1024)}, u32[]{:S(2)}) copy-start(f32[4096]{0:T(1024)} %param.10) | copy-start | bytes 49156
  25.1 4.8 %collective-permute-start.1 = (bf16[2,16,64,256]{3,2,0,1:T(8,128)(2,1)}, bf16[2,16,64,256]{3,2,0,1:T(8,128)(2,1)S(1)}, u32[]{:S(2)}, u32[]{:S(2)}) collective-permute-start(bf16[2,16,64,256]{3,2,0,1:T(8,128)(2,1)} %fusion.9), channel_id=1, source_target_pairs={{0,1},{1,0},{2,3},{3,2},{4,5},{5,4},{6,7},{7,6},{8,9},{9,8},{10,11... | collective-permute-start | bytes 3145736 | tf_op jit(solution)/shard_map/ppermute | solution.py:64
  30.3 43.4 %all-to-all-start = ((bf16[8,384,256]{2,1,0:T(8,128)(2,1)}), bf16[8,384,256]{2,1,0:T(8,128)(2,1)}, u32[]{:S(2)}, u32[]{:S(2)}) async-start(bf16[8,384,256]{2,1,0:T(8,128)(2,1)} %broadcast_in_dim.42), calls=%async_computation | async-start | bytes 3145728 | tf_op jit(solution)/shard_map/all_to_all | solution.py:73
  35.2 35.7 %collective-permute-start.2 = (bf16[16,64,256]{2,1,0:T(8,128)(2,1)S(1)}, bf16[16,64,256]{2,1,0:T(8,128)(2,1)S(1)}, u32[]{:S(2)}, u32[]{:S(2)}) collective-permute-start(bf16[16,64,256]{2,1,0:T(8,128)(2,1)S(1)} %fusion.11), channel_id=1, source_target_pairs={{0,2},{2,0},{1,3},{3,1},{4,6},{6,4},{5,7},{7,5},{8,10},{10,8},{9,1... | collective-permute-start | bytes 1572872 | tf_op jit(solution)/shard_map/ppermute | solution.py:75
  70.9 13.1 %collective-permute-start.3 = (bf16[16,64,256]{2,1,0:T(8,128)(2,1)S(1)}, bf16[16,64,256]{2,1,0:T(8,128)(2,1)S(1)}, u32[]{:S(2)}, u32[]{:S(2)}) collective-permute-start(bf16[16,64,256]{2,1,0:T(8,128)(2,1)S(1)} %bitcast.68), channel_id=1, source_target_pairs={{0,2},{2,0},{1,3},{3,1},{4,6},{6,4},{5,7},{7,5},{8,10},{10,8},{9,1... | collective-permute-start | bytes 1572872 | tf_op jit(solution)/shard_map/ppermute | solution.py:77
  73.8 35.4 %all-to-all-start.1 = ((bf16[16,64,256]{2,1,0:T(8,128)(2,1)}), bf16[16,64,256]{2,1,0:T(8,128)(2,1)S(1)}, u32[]{:S(2)}, u32[]{:S(2)}) async-start(bf16[16,64,256]{2,1,0:T(8,128)(2,1)} %add_convert_fusion.1), calls=%async_computation.1 | async-start | bytes 1048576 | tf_op jit(solution)/shard_map/all_to_all | solution.py:80
  82.1 4.4 %collective-permute-start.4 = (bf16[16,64,256]{2,1,0:T(8,128)(2,1)S(1)}, bf16[16,64,256]{2,1,0:T(8,128)(2,1)S(1)}, u32[]{:S(2)}, u32[]{:S(2)}) collective-permute-start(bf16[16,64,256]{2,1,0:T(8,128)(2,1)S(1)} %bitcast.69), channel_id=1, source_target_pairs={{0,1},{1,0},{2,3},{3,2},{4,5},{5,4},{6,7},{7,6},{8,9},{9,8},{10,11... | collective-permute-start | bytes 1572872 | tf_op jit(solution)/shard_map/ppermute | solution.py:78
  84.0 3.9 %collective-permute-start.5 = (bf16[16,64,256]{2,1,0:T(8,128)(2,1)S(1)}, bf16[16,64,256]{2,1,0:T(8,128)(2,1)S(1)}, u32[]{:S(2)}, u32[]{:S(2)}) collective-permute-start(bf16[16,64,256]{2,1,0:T(8,128)(2,1)S(1)} %collective-permute-done.3), channel_id=1, source_target_pairs={{0,1},{1,0},{2,3},{3,2},{4,5},{5,4},{6,7},{7,6},{8,9},{9,8},{10,11... | collective-permute-start | bytes 1572872 | tf_op jit(solution)/shard_map/ppermute | solution.py:82
  90.8 18.5 %copy-start.1 = (f32[64,256]{1,0:T(8,128)S(1)}, f32[64,256]{1,0:T(8,128)}, u32[]{:S(2)}) copy-start(f32[64,256]{1,0:T(8,128)} %param.11) | copy-start | bytes 196612
  90.8 18.5 %copy-start.3 = (f32[64,256]{1,0:T(8,128)S(1)}, f32[64,256]{1,0:T(8,128)}, u32[]{:S(2)}) copy-start(f32[64,256]{1,0:T(8,128)} %param.12) | copy-start | bytes 196612
  90.8 18.5 %copy-start.4 = (f32[64,256]{1,0:T(8,128)S(1)}, f32[64,256]{1,0:T(8,128)}, u32[]{:S(2)}) copy-start(f32[64,256]{1,0:T(8,128)} %param.13) | copy-start | bytes 196612
  102.2 7.0 %collective-permute-start.6 = (f32[3,128]{1,0:T(4,128)S(1)}, f32[3,128]{1,0:T(4,128)S(1)}, u32[]{:S(2)}, u32[]{:S(2)}) collective-permute-start(f32[3,128]{1,0:T(4,128)S(1)} %reduce_sum.38), channel_id=1, source_target_pairs={{0,256},{256,0},{1,257},{257,1},{2,258},{258,2},{3,259},{259,3},{4... | collective-permute-start | bytes 4616 | tf_op jit(solution)/shard_map/ppermute | solution.py:99

commit v5 on v4

--- a/solution.py
+++ b/solution.py
@@ -69,11 +69,12 @@
     halves = add_pair(keep, arrived).astype(jnp.bfloat16)
     keep = jnp.where(x_at == 0, halves[0], halves[1])
     give = jnp.where(x_at == 0, halves[1], halves[0])
-    give, keep, moved, kv_spread = lax.optimization_barrier((give, keep, moved, kv_spread))
+    give, keep, moved = lax.optimization_barrier((give, keep, moved))
+    kv_spread, _ = lax.optimization_barrier((kv_spread, give[0, 0, 0]))
     kv_all = lax.all_to_all(kv_spread, TENSOR, 0, 0)
     own_quarter = lax.all_gather(moved, "z", axis=0)
     arrived = lax.ppermute(give, "x_lo", SWAP)
-    arrived, own_quarter = lax.optimization_barrier((arrived, own_quarter))
+    arrived, _ = lax.optimization_barrier((arrived, own_quarter[0, 0, 0]))
     x_quarter = lax.ppermute(own_quarter, "x_lo", SWAP)
     core_quarter = lax.ppermute(own_quarter, "core", SWAP)
     quarters = add_pair(keep, arrived).astype(jnp.bfloat16)

time: 111 us -> 110 us (level)
  the two profiles are of different devices: /device:TPU:4 before, /device:TPU:32 now
where the time goes in v5:
time: 110 us; the launch traced here: 109 us
  starting transfers between devices  46.4 us (42%)
  blocking collectives  42.1 us (38%)
  other arithmetic  9.7 us (9%)
  matrix products  4.06 us (4%)
  waiting for transfers between devices  3.63 us (3%)
  local copies, waits for them, and re-layouts  2.46 us (2%)
    all_gather x1, blocking collectives, on_device(): own_quarter = lax.all_gather(moved, 'z', axis=0)  30.5 us
    all_to_all x1, starting transfers between devices, on_device(): kv_all = lax.all_to_all(kv_spread, TENSOR, 0, 0)  18.4 us
    all_gather x1, blocking collectives, on_device(): inner = jnp.sum(lax.all_gather(inner, 'y', axis=0), axis=0)  11.6 us
    all_to_all x1, starting transfers between devices, on_device(): planes = lax.all_to_all(quarters, 'z', 0, 0)  10.5 us
    ppermute x1, starting transfers between devices, on_device(): inner = inner + lax.ppermute(inner, 'x_hi', SWAP)  4.79 us
    ppermute x1, starting transfers between devices, on_device(): arrived = lax.ppermute(give, 'x_lo', SWAP)  3.4 us
    reduce_sum x1, other arithmetic, on_device(): jnp.mean(wide_rows * wide_rows, axis=-1, keepdims=True) + norm_eps  2.58 us
    ppermute x1, starting transfers between devices, on_device(): x_quarter = lax.ppermute(own_quarter, 'x_lo', SWAP)  2.43 us
  transfers between devices with their start and end apart: 9, of which 2 were waited for; matrix products, arithmetic and copies ran while one was open for 13% of the time, Pallas kernels for 0%

profile of v5, /device:TPU:32, one launch (start us, length us, event | category | flops | bytes accessed | tf_op | source)
XLA Modules:
  0.0 109.3 jit_solution(1983225801867746735)
XLA Ops:
  0.6 0.8 convert
  1.5 0.7 collective-permute-start
  2.2 2.3 %broadcast_in_dim.42 = bf16[8,384,256]{2,1,0:T(8,128)(2,1)} broadcast(bf16[384,256]{1,0:T(8,128)(2,1)} %bitcast.76), dimensions={1,2} | broadcast | bytes 1769472 | tf_op jit(solution)/shard_map/broadcast_in_dim | solution.py:44
  4.5 2.6 %fusion = f32[3,128]{1,0:T(4,128)S(1)} fusion(bf16[3,128,4096]{2,1,0:T(8,128)(2,1)} %param.8), kind=kLoop, calls=%fused_computation.2 | loop fusion | flops 4718208 | bytes 3147264 | tf_op jit(solution)/shard_map/reduce_sum | solution.py:51
  7.1 0.1 fusion.15
  7.2 1.6 %fusion.3 = bf16[4096,256]{1,0:T(8,128)(2,1)S(1)} fusion(bf16[3,128,4096]{2,1,0:T(8,128)(2,1)S(1)} %copy-done, f32[4096]{0:T(1024)S(1)} %copy-done.7, f32[3,128]{1,0:T(4,128)S(1)} %add_rsqrt_fusion, bf16[3,128,256]{2,1,0:T(8,128)(2,1)S(1)} %copy-done.2, pred[3,128]{1,0:T(4,128)(4,1)S(1)} %fusion.15), kind=kOutput, calls=%fused_computation.6 | convolution fusion | flops 812744704 | bytes 5457792 | tf_op jit(solution)/shard_map/dot_general | solution.py:53
  8.9 0.1 fusion.8
  9.0 1.1 %fusion.9 = bf16[2,16,64,256]{3,2,0,1:T(8,128)(2,1)} fusion(pred[]{:T(512)S(6)} %eq.7, bf16[2,2,16,64,256]{4,3,0,1,2:T(8,128)(2,1)S(1)} %bitcast.67), kind=kLoop, calls=%fused_computation.16 | loop fusion | flops 524288 | bytes 3145729 | tf_op jit(solution)/shard_map/jit(_where)/select_n | solution.py:61
  10.1 1.9 %collective-permute-start.1 = (bf16[2,16,64,256]{3,2,0,1:T(8,128)(2,1)}, bf16[2,16,64,256]{3,2,0,1:T(8,128)(2,1)S(1)}, u32[]{:S(2)}, u32[]{:S(2)}) collective-permute-start(bf16[2,16,64,256]{3,2,0,1:T(8,128)(2,1)} %fusion.9), channel_id=1, source_target_pairs={{0,1},{1,0},{2,3},{3,2},{4,5},{5,4},{6,7},{7,6},{8,9},{9,8},{10,11... | collective-permute-start | bytes 3145736 | tf_op jit(solution)/shard_map/ppermute | solution.py:64
  12.0 18.4 %all-to-all-start = ((bf16[8,384,256]{2,1,0:T(8,128)(2,1)}), bf16[8,384,256]{2,1,0:T(8,128)(2,1)}, u32[]{:S(2)}, u32[]{:S(2)}) async-start(bf16[8,384,256]{2,1,0:T(8,128)(2,1)} %broadcast_in_dim.42), calls=%async_computation | async-start | bytes 3145728 | tf_op jit(solution)/shard_map/all_to_all | solution.py:74
  30.4 1.1 %convert_multiply_fusion.2 = f32[3,128,512]{2,1,0:T(8,128)S(1)} fusion(f32[3,128]{1,0:T(4,128)S(1)} %add_rsqrt_fusion, bf16[3,128,4096]{2,1,0:T(8,128)(2,1)} %param.8, s32[]{:T(128)S(6)} %select_n.96), kind=kLoop, calls=%fused_computation.24 | loop fusion | flops 393216 | bytes 1181188 | tf_op jit(solution)/shard_map/mul | solution.py:66
  31.6 0.4 add_convert_fusion
  31.9 0.1 fusion.10
  32.1 3.4 %collective-permute-start.6 = (bf16[16,64,256]{2,1,0:T(8,128)(2,1)S(1)}, bf16[16,64,256]{2,1,0:T(8,128)(2,1)S(1)}, u32[]{:S(2)}, u32[]{:S(2)}) collective-permute-start(bf16[16,64,256]{2,1,0:T(8,128)(2,1)S(1)} %fusion.11), channel_id=1, source_target_pairs={{0,2},{2,0},{1,3},{3,1},{4,6},{6,4},{5,7},{7,5},{8,10},{10,8},{9,1... | collective-permute-start | bytes 1572872 | tf_op jit(solution)/shard_map/ppermute | solution.py:76
  35.5 30.5 %all-gather = bf16[1024,256]{1,0:T(8,128)(2,1)S(1)} all-gather(bf16[64,256]{1,0:T(8,128)(2,1)S(1)} %collective-permute-done), channel_id=2, replica_groups=mesh['x_hi'=2,'y'=4,'z'=16,'x_lo'=2,'core'=2] {'z'}, dimensions={0}, use_global_device_ids=true | all-gather | bytes 557056 | tf_op jit(solution)/shard_map/all_gather | solution.py:75
  66.0 2.4 %collective-permute-start.2 = (bf16[16,64,256]{2,1,0:T(8,128)(2,1)S(1)}, bf16[16,64,256]{2,1,0:T(8,128)(2,1)S(1)}, u32[]{:S(2)}, u32[]{:S(2)}) collective-permute-start(bf16[16,64,256]{2,1,0:T(8,128)(2,1)S(1)} %bitcast.68), channel_id=1, source_target_pairs={{0,2},{2,0},{1,3},{3,1},{4,6},{6,4},{5,7},{7,5},{8,10},{10,8},{9,1... | collective-permute-start | bytes 1572872 | tf_op jit(solution)/shard_map/ppermute | solution.py:78
  68.4 1.0 add_convert_fusion.1
  69.4 10.5 %all-to-all-start.1 = ((bf16[16,64,256]{2,1,0:T(8,128)(2,1)}), bf16[16,64,256]{2,1,0:T(8,128)(2,1)S(1)}, u32[]{:S(2)}, u32[]{:S(2)}) async-start(bf16[16,64,256]{2,1,0:T(8,128)(2,1)} %add_convert_fusion.1), calls=%async_computation.1 | async-start | bytes 1048576 | tf_op jit(solution)/shard_map/all_to_all | solution.py:81
  79.8 1.9 %collective-permute-start.3 = (bf16[16,64,256]{2,1,0:T(8,128)(2,1)S(1)}, bf16[16,64,256]{2,1,0:T(8,128)(2,1)S(1)}, u32[]{:S(2)}, u32[]{:S(2)}) collective-permute-start(bf16[16,64,256]{2,1,0:T(8,128)(2,1)S(1)} %bitcast.69), channel_id=1, source_target_pairs={{0,1},{1,0},{2,3},{3,2},{4,5},{5,4},{6,7},{7,6},{8,9},{9,8},{10,11... | collective-permute-start | bytes 1572872 | tf_op jit(solution)/shard_map/ppermute | solution.py:79
  81.8 2.4 %collective-permute-start.4 = (bf16[16,64,256]{2,1,0:T(8,128)(2,1)S(1)}, bf16[16,64,256]{2,1,0:T(8,128)(2,1)S(1)}, u32[]{:S(2)}, u32[]{:S(2)}) collective-permute-start(bf16[16,64,256]{2,1,0:T(8,128)(2,1)S(1)} %collective-permute-done.2), channel_id=1, source_target_pairs={{0,1},{1,0},{2,3},{3,2},{4,5},{5,4},{6,7},{7,6},{8,9},{9,8},{10,11... | collective-permute-start | bytes 1572872 | tf_op jit(solution)/shard_map/ppermute | solution.py:83
  84.2 0.1 dynamic_slice.7
  84.3 1.4 %collective-permute-done.4 = bf16[16,64,256]{2,1,0:T(8,128)(2,1)S(1)} collective-permute-done((bf16[16,64,256]{2,1,0:T(8,128)(2,1)S(1)}, bf16[16,64,256]{2,1,0:T(8,128)(2,1)S(1)}, u32[]{:S(2)}, u32[]{:S(2)}) %collective-permute-start.4) | collective-permute-done | bytes 524320 | tf_op jit(solution)/shard_map/ppermute | solution.py:83
  85.7 0.2 broadcast_select_fusion.7
  85.9 0.3 pad_maximum_fusion
  86.1 2.4 %fusion.7 = f32[3,128,512]{2,1,0:T(8,128)S(1)} fusion(bf16[3,128,8,256]{3,1,0,2:T(8,128)(2,1)} %bitcast.19, bf16[8,512,256,1]{2,1,3,0:T(8,128)(2,1)S(1)} %bitcast.71, f32[512]{0:T(512)S(1)} %dynamic_slice.7), kind=kOutput, calls=%fused_computation.13 | convolution fusion | flops 805502976 | bytes 4458496 | tf_op jit(solution)/shard_map/dot_general | solution.py:92
  88.6 0.3 multiply_select_fusion
  88.9 11.6 %all-gather.2 = f32[4,3,128]{2,1,0:T(4,128)S(1)} all-gather(f32[1,3,128]{2,1,0:T(4,128)S(1)} %bitcast.77), channel_id=3, replica_groups=mesh['x_hi'=2,'y'=4,'z'=16,'x_lo'=2,'core'=2] {'y'}, dimensions={0}, use_global_device_ids=true | all-gather | bytes 7680 | tf_op jit(solution)/shard_map/all_gather | solution.py:99
  100.6 4.8 %collective-permute-start.5 = (f32[3,128]{1,0:T(4,128)S(1)}, f32[3,128]{1,0:T(4,128)S(1)}, u32[]{:S(2)}, u32[]{:S(2)}) collective-permute-start(f32[3,128]{1,0:T(4,128)S(1)} %reduce_sum.38), channel_id=1, source_target_pairs={{0,256},{256,0},{1,257},{257,1},{2,258},{258,2},{3,259},{259,3},{4... | collective-permute-start | bytes 4616 | tf_op jit(solution)/shard_map/ppermute | solution.py:100
  105.4 2.2 %collective-permute-done.5 = f32[3,128]{1,0:T(4,128)S(1)} collective-permute-done((f32[3,128]{1,0:T(4,128)S(1)}, f32[3,128]{1,0:T(4,128)S(1)}, u32[]{:S(2)}, u32[]{:S(2)}) %collective-permute-start.5) | collective-permute-done | bytes 1568 | tf_op jit(solution)/shard_map/ppermute | solution.py:100
  107.6 0.1 convert_reduce_fusion
  107.7 0.7 divide_subtract_fusion
  108.4 0.9 subtract_convert_fusion
  (28 shorter events, 0.2 us)
Async XLA Ops:
  1.5 8.6 %collective-permute-start = (bf16[64,256]{1,0:T(8,128)(2,1)S(1)}, bf16[64,256]{1,0:T(8,128)(2,1)S(1)}, u32[]{:S(2)}, u32[]{:S(2)}) collective-permute-start(bf16[64,256]{1,0:T(8,128)(2,1)S(1)} %convert), channel_id=1, source_target_pairs={{0,0},{1,1},{2,2},{3,3},{4,4},{5,5},{6,6},{7,7},{8,64},{9,65},{10,... | collective-permute-start | bytes 98312 | tf_op jit(solution)/shard_map/ppermute | solution.py:42
  2.1 5.0 %copy-start.5 = (s32[3,128]{1,0:T(4,128)S(1)}, s32[3,128]{1,0:T(4,128)}, u32[]{:S(2)}) copy-start(s32[3,128]{1,0:T(4,128)} %param.15) | copy-start | bytes 4612
  2.2 5.0 %copy-start.6 = (s32[3,1]{0,1:T(1,128)S(1)}, s32[3,1]{0,1:T(1,128)}, u32[]{:S(2)}) copy-start(s32[3,1]{0,1:T(1,128)} %param.14) | copy-start | bytes 40
  2.2 5.1 %copy-start = (bf16[3,128,4096]{2,1,0:T(8,128)(2,1)S(1)}, bf16[3,128,4096]{2,1,0:T(8,128)(2,1)}, u32[]{:S(2)}) copy-start(bf16[3,128,4096]{2,1,0:T(8,128)(2,1)} %param.8) | copy-start | bytes 9437188
  2.2 5.0 %copy-start.2 = (bf16[3,128,256]{2,1,0:T(8,128)(2,1)S(1)}, bf16[3,128,256]{2,1,0:T(8,128)(2,1)}, u32[]{:S(2)}) copy-start(bf16[3,128,256]{2,1,0:T(8,128)(2,1)} %param.9) | copy-start | bytes 589828
  2.2 5.0 %copy-start.7 = (f32[4096]{0:T(1024)S(1)}, f32[4096]{0:T(1024)}, u32[]{:S(2)}) copy-start(f32[4096]{0:T(1024)} %param.10) | copy-start | bytes 49156
  10.1 21.5 %collective-permute-start.1 = (bf16[2,16,64,256]{3,2,0,1:T(8,128)(2,1)}, bf16[2,16,64,256]{3,2,0,1:T(8,128)(2,1)S(1)}, u32[]{:S(2)}, u32[]{:S(2)}) collective-permute-start(bf16[2,16,64,256]{3,2,0,1:T(8,128)(2,1)} %fusion.9), channel_id=1, source_target_pairs={{0,1},{1,0},{2,3},{3,2},{4,5},{5,4},{6,7},{7,6},{8,9},{9,8},{10,11... | collective-permute-start | bytes 3145736 | tf_op jit(solution)/shard_map/ppermute | solution.py:64
  12.0 57.4 %all-to-all-start = ((bf16[8,384,256]{2,1,0:T(8,128)(2,1)}), bf16[8,384,256]{2,1,0:T(8,128)(2,1)}, u32[]{:S(2)}, u32[]{:S(2)}) async-start(bf16[8,384,256]{2,1,0:T(8,128)(2,1)} %broadcast_in_dim.42), calls=%async_computation | async-start | bytes 3145728 | tf_op jit(solution)/shard_map/all_to_all | solution.py:74
  32.1 36.3 %collective-permute-start.6 = (bf16[16,64,256]{2,1,0:T(8,128)(2,1)S(1)}, bf16[16,64,256]{2,1,0:T(8,128)(2,1)S(1)}, u32[]{:S(2)}, u32[]{:S(2)}) collective-permute-start(bf16[16,64,256]{2,1,0:T(8,128)(2,1)S(1)} %fusion.11), channel_id=1, source_target_pairs={{0,2},{2,0},{1,3},{3,1},{4,6},{6,4},{5,7},{7,5},{8,10},{10,8},{9,1... | collective-permute-start | bytes 1572872 | tf_op jit(solution)/shard_map/ppermute | solution.py:76
  66.0 15.8 %collective-permute-start.2 = (bf16[16,64,256]{2,1,0:T(8,128)(2,1)S(1)}, bf16[16,64,256]{2,1,0:T(8,128)(2,1)S(1)}, u32[]{:S(2)}, u32[]{:S(2)}) collective-permute-start(bf16[16,64,256]{2,1,0:T(8,128)(2,1)S(1)} %bitcast.68), channel_id=1, source_target_pairs={{0,2},{2,0},{1,3},{3,1},{4,6},{6,4},{5,7},{7,5},{8,10},{10,8},{9,1... | collective-permute-start | bytes 1572872 | tf_op jit(solution)/shard_map/ppermute | solution.py:78
  69.4 38.2 %all-to-all-start.1 = ((bf16[16,64,256]{2,1,0:T(8,128)(2,1)}), bf16[16,64,256]{2,1,0:T(8,128)(2,1)S(1)}, u32[]{:S(2)}, u32[]{:S(2)}) async-start(bf16[16,64,256]{2,1,0:T(8,128)(2,1)} %add_convert_fusion.1), calls=%async_computation.1 | async-start | bytes 1048576 | tf_op jit(solution)/shard_map/all_to_all | solution.py:81
  79.8 4.4 %collective-permute-start.3 = (bf16[16,64,256]{2,1,0:T(8,128)(2,1)S(1)}, bf16[16,64,256]{2,1,0:T(8,128)(2,1)S(1)}, u32[]{:S(2)}, u32[]{:S(2)}) collective-permute-start(bf16[16,64,256]{2,1,0:T(8,128)(2,1)S(1)} %bitcast.69), channel_id=1, source_target_pairs={{0,1},{1,0},{2,3},{3,2},{4,5},{5,4},{6,7},{7,6},{8,9},{9,8},{10,11... | collective-permute-start | bytes 1572872 | tf_op jit(solution)/shard_map/ppermute | solution.py:79
  81.8 3.9 %collective-permute-start.4 = (bf16[16,64,256]{2,1,0:T(8,128)(2,1)S(1)}, bf16[16,64,256]{2,1,0:T(8,128)(2,1)S(1)}, u32[]{:S(2)}, u32[]{:S(2)}) collective-permute-start(bf16[16,64,256]{2,1,0:T(8,128)(2,1)S(1)} %collective-permute-done.2), channel_id=1, source_target_pairs={{0,1},{1,0},{2,3},{3,2},{4,5},{5,4},{6,7},{7,6},{8,9},{9,8},{10,11... | collective-permute-start | bytes 1572872 | tf_op jit(solution)/shard_map/ppermute | solution.py:83
  88.6 19.1 %copy-start.1 = (f32[64,256]{1,0:T(8,128)S(1)}, f32[64,256]{1,0:T(8,128)}, u32[]{:S(2)}) copy-start(f32[64,256]{1,0:T(8,128)} %param.11) | copy-start | bytes 196612
  88.6 19.1 %copy-start.3 = (f32[64,256]{1,0:T(8,128)S(1)}, f32[64,256]{1,0:T(8,128)}, u32[]{:S(2)}) copy-start(f32[64,256]{1,0:T(8,128)} %param.12) | copy-start | bytes 196612
  88.6 19.1 %copy-start.4 = (f32[64,256]{1,0:T(8,128)S(1)}, f32[64,256]{1,0:T(8,128)}, u32[]{:S(2)}) copy-start(f32[64,256]{1,0:T(8,128)} %param.13) | copy-start | bytes 196612
  100.6 7.0 %collective-permute-start.5 = (f32[3,128]{1,0:T(4,128)S(1)}, f32[3,128]{1,0:T(4,128)S(1)}, u32[]{:S(2)}, u32[]{:S(2)}) collective-permute-start(f32[3,128]{1,0:T(4,128)S(1)} %reduce_sum.38), channel_id=1, source_target_pairs={{0,256},{256,0},{1,257},{257,1},{2,258},{258,2},{3,259},{259,3},{4... | collective-permute-start | bytes 4616 | tf_op jit(solution)/shard_map/ppermute | solution.py:100

commit v6 on v5

--- a/solution.py
+++ b/solution.py
@@ -96,8 +96,8 @@
     slice_gain = lax.dynamic_slice_in_dim(norm_gain, offset, 512, 0)
     scaled = normed_grad * slice_gain
     inner = jnp.sum(scaled * slice_unit, axis=-1)
+    inner = inner + lax.ppermute(inner, "x_hi", SWAP)
     inner = jnp.sum(lax.all_gather(inner, "y", axis=0), axis=0)
-    inner = inner + lax.ppermute(inner, "x_hi", SWAP)
     weight_grad = jnp.sum(planes.astype(jnp.float32), axis=0)
     mean_grad = weight_grad / 64**0.5
     new_moment_one = beta_one * moment_one + (1.0 - beta_one) * mean_grad

time: 110 us -> 110 us (level)
  no operation moved by 1% of the time
where the time goes in v6:
time: 110 us; the launch traced here: 109 us
  starting transfers between devices  47 us (43%)
  blocking collectives  42.1 us (38%)
  other arithmetic  9.7 us (9%)
  matrix products  4.06 us (4%)
  waiting for transfers between devices  3.03 us (3%)
  local copies, waits for them, and re-layouts  2.46 us (2%)
    all_gather x1, blocking collectives, on_device(): own_quarter = lax.all_gather(moved, 'z', axis=0)  30.5 us
    all_to_all x1, starting transfers between devices, on_device(): kv_all = lax.all_to_all(kv_spread, TENSOR, 0, 0)  18.4 us
    all_gather x1, blocking collectives, on_device(): inner = jnp.sum(lax.all_gather(inner, 'y', axis=0), axis=0)  11.6 us
    all_to_all x1, starting transfers between devices, on_device(): planes = lax.all_to_all(quarters, 'z', 0, 0)  10.5 us
    ppermute x1, starting transfers between devices, on_device(): inner = inner + lax.ppermute(inner, 'x_hi', SWAP)  5.4 us
    ppermute x1, starting transfers between devices, on_device(): arrived = lax.ppermute(give, 'x_lo', SWAP)  3.4 us
    reduce_sum x1, other arithmetic, on_device(): jnp.mean(wide_rows * wide_rows, axis=-1, keepdims=True) + norm_eps  2.58 us
    ppermute x1, starting transfers between devices, on_device(): x_quarter = lax.ppermute(own_quarter, 'x_lo', SWAP)  2.43 us
  transfers between devices with their start and end apart: 9, of which 2 were waited for; matrix products, arithmetic and copies ran while one was open for 13% of the time, Pallas kernels for 0%

profile of v6, /device:TPU:32, one launch (start us, length us, event | category | flops | bytes accessed | tf_op | source)
XLA Modules:
  0.0 109.3 jit_solution(4030739105964139106)
XLA Ops:
  0.6 0.8 convert
  1.5 0.7 collective-permute-start
  2.2 2.3 %broadcast_in_dim.42 = bf16[8,384,256]{2,1,0:T(8,128)(2,1)} broadcast(bf16[384,256]{1,0:T(8,128)(2,1)} %bitcast.77), dimensions={1,2} | broadcast | bytes 1769472 | tf_op jit(solution)/shard_map/broadcast_in_dim | solution.py:44
  4.5 2.6 %fusion = f32[3,128]{1,0:T(4,128)S(1)} fusion(bf16[3,128,4096]{2,1,0:T(8,128)(2,1)} %param.8), kind=kLoop, calls=%fused_computation.2 | loop fusion | flops 4718208 | bytes 3147264 | tf_op jit(solution)/shard_map/reduce_sum | solution.py:51
  7.1 0.1 fusion.15
  7.2 1.6 %fusion.3 = bf16[4096,256]{1,0:T(8,128)(2,1)S(1)} fusion(bf16[3,128,4096]{2,1,0:T(8,128)(2,1)S(1)} %copy-done, f32[4096]{0:T(1024)S(1)} %copy-done.7, f32[3,128]{1,0:T(4,128)S(1)} %add_rsqrt_fusion, bf16[3,128,256]{2,1,0:T(8,128)(2,1)S(1)} %copy-done.2, pred[3,128]{1,0:T(4,128)(4,1)S(1)} %fusion.15), kind=kOutput, calls=%fused_computation.6 | convolution fusion | flops 812744704 | bytes 5457792 | tf_op jit(solution)/shard_map/dot_general | solution.py:53
  8.9 0.1 fusion.8
  9.0 1.1 %fusion.9 = bf16[2,16,64,256]{3,2,0,1:T(8,128)(2,1)} fusion(pred[]{:T(512)S(6)} %eq.7, bf16[2,2,16,64,256]{4,3,0,1,2:T(8,128)(2,1)S(1)} %bitcast.68), kind=kLoop, calls=%fused_computation.16 | loop fusion | flops 524288 | bytes 3145729 | tf_op jit(solution)/shard_map/jit(_where)/select_n | solution.py:61
  10.1 1.9 %collective-permute-start.1 = (bf16[2,16,64,256]{3,2,0,1:T(8,128)(2,1)}, bf16[2,16,64,256]{3,2,0,1:T(8,128)(2,1)S(1)}, u32[]{:S(2)}, u32[]{:S(2)}) collective-permute-start(bf16[2,16,64,256]{3,2,0,1:T(8,128)(2,1)} %fusion.9), channel_id=1, source_target_pairs={{0,1},{1,0},{2,3},{3,2},{4,5},{5,4},{6,7},{7,6},{8,9},{9,8},{10,11... | collective-permute-start | bytes 3145736 | tf_op jit(solution)/shard_map/ppermute | solution.py:64
  12.0 18.4 %all-to-all-start = ((bf16[8,384,256]{2,1,0:T(8,128)(2,1)}), bf16[8,384,256]{2,1,0:T(8,128)(2,1)}, u32[]{:S(2)}, u32[]{:S(2)}) async-start(bf16[8,384,256]{2,1,0:T(8,128)(2,1)} %broadcast_in_dim.42), calls=%async_computation | async-start | bytes 3145728 | tf_op jit(solution)/shard_map/all_to_all | solution.py:74
  30.4 1.1 %convert_multiply_fusion.2 = f32[3,128,512]{2,1,0:T(8,128)S(1)} fusion(f32[3,128]{1,0:T(4,128)S(1)} %add_rsqrt_fusion, bf16[3,128,4096]{2,1,0:T(8,128)(2,1)} %param.8, s32[]{:T(128)S(6)} %select_n.96), kind=kLoop, calls=%fused_computation.24 | loop fusion | flops 393216 | bytes 1181188 | tf_op jit(solution)/shard_map/mul | solution.py:66
  31.6 0.4 add_convert_fusion
  31.9 0.1 fusion.10
  32.1 3.4 %collective-permute-start.6 = (bf16[16,64,256]{2,1,0:T(8,128)(2,1)S(1)}, bf16[16,64,256]{2,1,0:T(8,128)(2,1)S(1)}, u32[]{:S(2)}, u32[]{:S(2)}) collective-permute-start(bf16[16,64,256]{2,1,0:T(8,128)(2,1)S(1)} %fusion.11), channel_id=1, source_target_pairs={{0,2},{2,0},{1,3},{3,1},{4,6},{6,4},{5,7},{7,5},{8,10},{10,8},{9,1... | collective-permute-start | bytes 1572872 | tf_op jit(solution)/shard_map/ppermute | solution.py:76
  35.5 30.5 %all-gather = bf16[1024,256]{1,0:T(8,128)(2,1)S(1)} all-gather(bf16[64,256]{1,0:T(8,128)(2,1)S(1)} %collective-permute-done), channel_id=2, replica_groups=mesh['x_hi'=2,'y'=4,'z'=16,'x_lo'=2,'core'=2] {'z'}, dimensions={0}, use_global_device_ids=true | all-gather | bytes 557056 | tf_op jit(solution)/shard_map/all_gather | solution.py:75
  66.0 2.4 %collective-permute-start.2 = (bf16[16,64,256]{2,1,0:T(8,128)(2,1)S(1)}, bf16[16,64,256]{2,1,0:T(8,128)(2,1)S(1)}, u32[]{:S(2)}, u32[]{:S(2)}) collective-permute-start(bf16[16,64,256]{2,1,0:T(8,128)(2,1)S(1)} %bitcast.69), channel_id=1, source_target_pairs={{0,2},{2,0},{1,3},{3,1},{4,6},{6,4},{5,7},{7,5},{8,10},{10,8},{9,1... | collective-permute-start | bytes 1572872 | tf_op jit(solution)/shard_map/ppermute | solution.py:78
  68.4 1.0 add_convert_fusion.1
  69.4 10.5 %all-to-all-start.1 = ((bf16[16,64,256]{2,1,0:T(8,128)(2,1)}), bf16[16,64,256]{2,1,0:T(8,128)(2,1)S(1)}, u32[]{:S(2)}, u32[]{:S(2)}) async-start(bf16[16,64,256]{2,1,0:T(8,128)(2,1)} %add_convert_fusion.1), calls=%async_computation.1 | async-start | bytes 1048576 | tf_op jit(solution)/shard_map/all_to_all | solution.py:81
  79.8 1.9 %collective-permute-start.3 = (bf16[16,64,256]{2,1,0:T(8,128)(2,1)S(1)}, bf16[16,64,256]{2,1,0:T(8,128)(2,1)S(1)}, u32[]{:S(2)}, u32[]{:S(2)}) collective-permute-start(bf16[16,64,256]{2,1,0:T(8,128)(2,1)S(1)} %bitcast.70), channel_id=1, source_target_pairs={{0,1},{1,0},{2,3},{3,2},{4,5},{5,4},{6,7},{7,6},{8,9},{9,8},{10,11... | collective-permute-start | bytes 1572872 | tf_op jit(solution)/shard_map/ppermute | solution.py:79
  81.8 2.4 %collective-permute-start.4 = (bf16[16,64,256]{2,1,0:T(8,128)(2,1)S(1)}, bf16[16,64,256]{2,1,0:T(8,128)(2,1)S(1)}, u32[]{:S(2)}, u32[]{:S(2)}) collective-permute-start(bf16[16,64,256]{2,1,0:T(8,128)(2,1)S(1)} %collective-permute-done.2), channel_id=1, source_target_pairs={{0,1},{1,0},{2,3},{3,2},{4,5},{5,4},{6,7},{7,6},{8,9},{9,8},{10,11... | collective-permute-start | bytes 1572872 | tf_op jit(solution)/shard_map/ppermute | solution.py:83
  84.2 0.1 dynamic_slice.7
  84.3 1.4 %collective-permute-done.4 = bf16[16,64,256]{2,1,0:T(8,128)(2,1)S(1)} collective-permute-done((bf16[16,64,256]{2,1,0:T(8,128)(2,1)S(1)}, bf16[16,64,256]{2,1,0:T(8,128)(2,1)S(1)}, u32[]{:S(2)}, u32[]{:S(2)}) %collective-permute-start.4) | collective-permute-done | bytes 524320 | tf_op jit(solution)/shard_map/ppermute | solution.py:83
  85.7 0.2 broadcast_select_fusion.7
  85.9 0.3 pad_maximum_fusion
  86.1 2.4 %fusion.7 = f32[3,128,512]{2,1,0:T(8,128)S(1)} fusion(bf16[3,128,8,256]{3,1,0,2:T(8,128)(2,1)} %bitcast.19, bf16[8,512,256,1]{2,1,3,0:T(8,128)(2,1)S(1)} %bitcast.72, f32[512]{0:T(512)S(1)} %dynamic_slice.7), kind=kOutput, calls=%fused_computation.13 | convolution fusion | flops 805502976 | bytes 4458496 | tf_op jit(solution)/shard_map/dot_general | solution.py:92
  88.6 0.3 multiply_select_fusion
  88.9 5.4 %collective-permute-start.5 = (f32[3,128]{1,0:T(4,128)S(1)}, f32[3,128]{1,0:T(4,128)S(1)}, u32[]{:S(2)}, u32[]{:S(2)}) collective-permute-start(f32[3,128]{1,0:T(4,128)S(1)} %get-tuple-element.50), channel_id=1, source_target_pairs={{0,256},{256,0},{1,257},{257,1},{2,258},{258,2},{3,259},{259,3},{4... | collective-permute-start | bytes 4616 | tf_op jit(solution)/shard_map/ppermute | solution.py:99
  94.3 1.6 %collective-permute-done.5 = f32[3,128]{1,0:T(4,128)S(1)} collective-permute-done((f32[3,128]{1,0:T(4,128)S(1)}, f32[3,128]{1,0:T(4,128)S(1)}, u32[]{:S(2)}, u32[]{:S(2)}) %collective-permute-start.5) | collective-permute-done | bytes 1568 | tf_op jit(solution)/shard_map/ppermute | solution.py:99
  95.9 11.6 %all-gather.2 = f32[4,3,128]{2,1,0:T(4,128)S(1)} all-gather(f32[1,3,128]{2,1,0:T(4,128)S(1)} %add_bitcast_fusion), channel_id=3, replica_groups=mesh['x_hi'=2,'y'=4,'z'=16,'x_lo'=2,'core'=2] {'y'}, dimensions={0}, use_global_device_ids=true | all-gather | bytes 7680 | tf_op jit(solution)/shard_map/all_gather | solution.py:100
  107.6 0.1 convert_reduce_fusion
  107.7 0.7 divide_subtract_fusion
  108.4 0.9 subtract_convert_fusion
  (28 shorter events, 0.2 us)
Async XLA Ops:
  1.5 8.6 %collective-permute-start = (bf16[64,256]{1,0:T(8,128)(2,1)S(1)}, bf16[64,256]{1,0:T(8,128)(2,1)S(1)}, u32[]{:S(2)}, u32[]{:S(2)}) collective-permute-start(bf16[64,256]{1,0:T(8,128)(2,1)S(1)} %convert), channel_id=1, source_target_pairs={{0,0},{1,1},{2,2},{3,3},{4,4},{5,5},{6,6},{7,7},{8,64},{9,65},{10,... | collective-permute-start | bytes 98312 | tf_op jit(solution)/shard_map/ppermute | solution.py:42
  2.1 5.0 %copy-start.5 = (s32[3,128]{1,0:T(4,128)S(1)}, s32[3,128]{1,0:T(4,128)}, u32[]{:S(2)}) copy-start(s32[3,128]{1,0:T(4,128)} %param.15) | copy-start | bytes 4612
  2.2 5.0 %copy-start.6 = (s32[3,1]{0,1:T(1,128)S(1)}, s32[3,1]{0,1:T(1,128)}, u32[]{:S(2)}) copy-start(s32[3,1]{0,1:T(1,128)} %param.14) | copy-start | bytes 40
  2.2 5.1 %copy-start = (bf16[3,128,4096]{2,1,0:T(8,128)(2,1)S(1)}, bf16[3,128,4096]{2,1,0:T(8,128)(2,1)}, u32[]{:S(2)}) copy-start(bf16[3,128,4096]{2,1,0:T(8,128)(2,1)} %param.8) | copy-start | bytes 9437188
  2.2 5.0 %copy-start.2 = (bf16[3,128,256]{2,1,0:T(8,128)(2,1)S(1)}, bf16[3,128,256]{2,1,0:T(8,128)(2,1)}, u32[]{:S(2)}) copy-start(bf16[3,128,256]{2,1,0:T(8,128)(2,1)} %param.9) | copy-start | bytes 589828
  2.2 5.0 %copy-start.7 = (f32[4096]{0:T(1024)S(1)}, f32[4096]{0:T(1024)}, u32[]{:S(2)}) copy-start(f32[4096]{0:T(1024)} %param.10) | copy-start | bytes 49156
  10.1 21.5 %collective-permute-start.1 = (bf16[2,16,64,256]{3,2,0,1:T(8,128)(2,1)}, bf16[2,16,64,256]{3,2,0,1:T(8,128)(2,1)S(1)}, u32[]{:S(2)}, u32[]{:S(2)}) collective-permute-start(bf16[2,16,64,256]{3,2,0,1:T(8,128)(2,1)} %fusion.9), channel_id=1, source_target_pairs={{0,1},{1,0},{2,3},{3,2},{4,5},{5,4},{6,7},{7,6},{8,9},{9,8},{10,11... | collective-permute-start | bytes 3145736 | tf_op jit(solution)/shard_map/ppermute | solution.py:64
  12.0 57.4 %all-to-all-start = ((bf16[8,384,256]{2,1,0:T(8,128)(2,1)}), bf16[8,384,256]{2,1,0:T(8,128)(2,1)}, u32[]{:S(2)}, u32[]{:S(2)}) async-start(bf16[8,384,256]{2,1,0:T(8,128)(2,1)} %broadcast_in_dim.42), calls=%async_computation | async-start | bytes 3145728 | tf_op jit(solution)/shard_map/all_to_all | solution.py:74
  32.1 36.3 %collective-permute-start.6 = (bf16[16,64,256]{2,1,0:T(8,128)(2,1)S(1)}, bf16[16,64,256]{2,1,0:T(8,128)(2,1)S(1)}, u32[]{:S(2)}, u32[]{:S(2)}) collective-permute-start(bf16[16,64,256]{2,1,0:T(8,128)(2,1)S(1)} %fusion.11), channel_id=1, source_target_pairs={{0,2},{2,0},{1,3},{3,1},{4,6},{6,4},{5,7},{7,5},{8,10},{10,8},{9,1... | collective-permute-start | bytes 1572872 | tf_op jit(solution)/shard_map/ppermute | solution.py:76
  66.0 15.8 %collective-permute-start.2 = (bf16[16,64,256]{2,1,0:T(8,128)(2,1)S(1)}, bf16[16,64,256]{2,1,0:T(8,128)(2,1)S(1)}, u32[]{:S(2)}, u32[]{:S(2)}) collective-permute-start(bf16[16,64,256]{2,1,0:T(8,128)(2,1)S(1)} %bitcast.69), channel_id=1, source_target_pairs={{0,2},{2,0},{1,3},{3,1},{4,6},{6,4},{5,7},{7,5},{8,10},{10,8},{9,1... | collective-permute-start | bytes 1572872 | tf_op jit(solution)/shard_map/ppermute | solution.py:78
  69.4 38.2 %all-to-all-start.1 = ((bf16[16,64,256]{2,1,0:T(8,128)(2,1)}), bf16[16,64,256]{2,1,0:T(8,128)(2,1)S(1)}, u32[]{:S(2)}, u32[]{:S(2)}) async-start(bf16[16,64,256]{2,1,0:T(8,128)(2,1)} %add_convert_fusion.1), calls=%async_computation.1 | async-start | bytes 1048576 | tf_op jit(solution)/shard_map/all_to_all | solution.py:81
  79.8 4.4 %collective-permute-start.3 = (bf16[16,64,256]{2,1,0:T(8,128)(2,1)S(1)}, bf16[16,64,256]{2,1,0:T(8,128)(2,1)S(1)}, u32[]{:S(2)}, u32[]{:S(2)}) collective-permute-start(bf16[16,64,256]{2,1,0:T(8,128)(2,1)S(1)} %bitcast.70), channel_id=1, source_target_pairs={{0,1},{1,0},{2,3},{3,2},{4,5},{5,4},{6,7},{7,6},{8,9},{9,8},{10,11... | collective-permute-start | bytes 1572872 | tf_op jit(solution)/shard_map/ppermute | solution.py:79
  81.8 3.9 %collective-permute-start.4 = (bf16[16,64,256]{2,1,0:T(8,128)(2,1)S(1)}, bf16[16,64,256]{2,1,0:T(8,128)(2,1)S(1)}, u32[]{:S(2)}, u32[]{:S(2)}) collective-permute-start(bf16[16,64,256]{2,1,0:T(8,128)(2,1)S(1)} %collective-permute-done.2), channel_id=1, source_target_pairs={{0,1},{1,0},{2,3},{3,2},{4,5},{5,4},{6,7},{7,6},{8,9},{9,8},{10,11... | collective-permute-start | bytes 1572872 | tf_op jit(solution)/shard_map/ppermute | solution.py:83
  88.6 19.1 %copy-start.1 = (f32[64,256]{1,0:T(8,128)S(1)}, f32[64,256]{1,0:T(8,128)}, u32[]{:S(2)}) copy-start(f32[64,256]{1,0:T(8,128)} %param.11) | copy-start | bytes 196612
  88.6 19.1 %copy-start.3 = (f32[64,256]{1,0:T(8,128)S(1)}, f32[64,256]{1,0:T(8,128)}, u32[]{:S(2)}) copy-start(f32[64,256]{1,0:T(8,128)} %param.12) | copy-start | bytes 196612
  88.6 19.1 %copy-start.4 = (f32[64,256]{1,0:T(8,128)S(1)}, f32[64,256]{1,0:T(8,128)}, u32[]{:S(2)}) copy-start(f32[64,256]{1,0:T(8,128)} %param.13) | copy-start | bytes 196612
  88.9 7.0 %collective-permute-start.5 = (f32[3,128]{1,0:T(4,128)S(1)}, f32[3,128]{1,0:T(4,128)S(1)}, u32[]{:S(2)}, u32[]{:S(2)}) collective-permute-start(f32[3,128]{1,0:T(4,128)S(1)} %get-tuple-element.50), channel_id=1, source_target_pairs={{0,256},{256,0},{1,257},{257,1},{2,258},{258,2},{3,259},{259,3},{4... | collective-permute-start | bytes 4616 | tf_op jit(solution)/shard_map/ppermute | solution.py:99
